TPU v7x, 256 devices: a whole 4x4x8 slice. The times are simulated.
256 devices in a mesh: vel: 16 (over z_lo, x), gx: 8 (over y, core), gy: 2 (over z_hi).
Axes of the slice: x: 4, y: 4, z: 8 (z_hi: 2, z_lo: 4; z = z_hi * 4 + z_lo), core: 2. Of those that a mesh axis runs over, the one named last changes fastest.
Arguments:
- dist: float32 [3, 3, 128, 64, 4096], P(None, None, 'gx', 'gy', 'vel'), as said below
- cell_kind: int32 [128, 64], replicated, may hold values from 0 to 1, as said below
- inflow: float32 [4096], P('vel'), may hold values from 0.05 to 1.5
Outputs:
- dist_next: float32 [3, 3, 128, 64, 4096], P(None, None, 'gx', 'gy', 'vel')
- node_fields: float32 [5, 3, 3, 128, 64], P(None, None, None, 'gx', 'gy')
Inputs may be any that keep to these rules, and one draw needn't show every extreme that they name: `dist`: every entry is positive. `cell_kind`: the ones form a single disc of elements that touches no edge of the grid.
All inputs are finite; a program needn't handle non-finite values.
Results may differ from a plain program's by a relative error of at most 0.00013.
Values sent between devices are 32-bit elements; how exact they have to be, the bound alone decides.
No kernel may reach another device: no remote copies, remote signals or barrier semaphores. Data moves between devices by JAX's collectives and lax.ppermute only.
A program may use at most 128 MiB of HBM per device.

v0:
```python
import math

import jax
import jax.numpy as jnp
from jax import lax
from jax.sharding import PartitionSpec as P

NV = 16


vel_max = 5.0
rarefaction_ratio = 0.25
time_step = 0.08


def extended(block, sides, width):
    for axis, dim in sides:
        count = lax.axis_size(axis)
        forward = [(i, i + 1) for i in range(count - 1)]
        backward = [(target, source) for source, target in forward]
        low = lax.ppermute(
            lax.slice_in_dim(block, block.shape[dim] - width, None, axis=dim), axis, forward
        )
        high = lax.ppermute(lax.slice_in_dim(block, 0, width, axis=dim), axis, backward)
        block = jnp.concatenate([low, block, high], axis=dim)
    return block


def velocity_grid(index):
    spacing = 2.0 * vel_max / NV

    def coordinate(level):
        return (level.astype(jnp.float32) + 0.5) * spacing - vel_max

    return (coordinate(index // (NV * NV)), coordinate(index // NV % NV), coordinate(index % NV))


def quad_weight():
    spacing = 2.0 * vel_max / NV
    return spacing**3 / (2.0 * math.pi) ** 1.5


def moment_rows(index):
    speed_x, speed_y, speed_z = velocity_grid(index)
    weights = [
        jnp.ones_like(speed_x),
        speed_x,
        speed_y,
        speed_z,
        0.5 * (speed_x * speed_x + speed_y * speed_y + speed_z * speed_z),
        jnp.maximum(-speed_x, 0.0),
        jnp.maximum(speed_x, 0.0),
        jnp.maximum(-speed_y, 0.0),
        jnp.maximum(speed_y, 0.0),
    ]
    return quad_weight() * jnp.stack(weights)


def wall_scale():
    speed_x, speed_y, speed_z = velocity_grid(jnp.arange(NV * NV * NV, dtype=jnp.int32))
    energy = speed_x * speed_x + speed_y * speed_y + speed_z * speed_z
    return jnp.sum(quad_weight() * jnp.maximum(-speed_x, 0.0) * jnp.exp(-0.5 * energy))


def split_sums(totals):
    fluid_averages = totals[:5]
    exit_edge_condition = jnp.stack([totals[5][0], totals[6][2], totals[7][:, 0], totals[8][:, 2]])
    return (fluid_averages, exit_edge_condition)


def parameters(fluid_averages, exit_edge_condition, heat_speed_factor):
    particle_crowding = fluid_averages[0]
    mean_flow_first_axis = fluid_averages[1] / particle_crowding
    mean_flow_second_axis = fluid_averages[2] / particle_crowding
    mean_flow_third_axis = fluid_averages[3] / particle_crowding
    kinetic_heat_level = (
        2.0
        / 3.0
        * (
            fluid_averages[4] / particle_crowding
            - 0.5
            * (
                mean_flow_first_axis * mean_flow_first_axis
                + mean_flow_second_axis * mean_flow_second_axis
                + mean_flow_third_axis * mean_flow_third_axis
            )
        )
    )
    return (
        jnp.stack(
            [
                particle_crowding,
                mean_flow_first_axis,
                mean_flow_second_axis,
                mean_flow_third_axis,
                kinetic_heat_level,
            ]
        ),
        exit_edge_condition / heat_speed_factor,
    )


def derivative(field, axis):
    first = lax.index_in_dim(field, 0, axis)
    middle = lax.index_in_dim(field, 1, axis)
    final = lax.index_in_dim(field, 2, axis)
    return jnp.concatenate(
        [
            -1.5 * first + 2.0 * middle - 0.5 * final,
            0.5 * (final - first),
            0.5 * first - 2.0 * middle + 1.5 * final,
        ],
        axis,
    )


def neighbor_kinds(cell_kind, start_x, start_y, width_x, width_y):
    padded = jnp.pad(cell_kind, 1)

    def window(off_x, off_y):
        return lax.dynamic_slice(padded, (start_x + off_x, start_y + off_y), (width_x, width_y))[
            :, :, None
        ]

    return (window(1, 1), window(0, 1), window(2, 1), window(1, 0), window(1, 2))


def edge_masks(start_x, start_y, width_x, width_y, total_x, total_y):
    column = start_x + jnp.arange(width_x, dtype=jnp.int32)
    row_pos = start_y + jnp.arange(width_y, dtype=jnp.int32)
    return (
        (column == 0)[:, None, None],
        (column == total_x - 1)[:, None, None],
        (row_pos == 0)[None, :, None],
        (row_pos == total_y - 1)[None, :, None],
    )


def section(planes, index, inflow_part, node_fields, wall_density, kinds, edges, raw):
    speed_x, speed_y, speed_z = velocity_grid(index)
    energy = speed_x * speed_x + speed_y * speed_y + speed_z * speed_z
    wall_shape = jnp.exp(-0.5 * energy)
    own_kind, kind_left, kind_right, kind_below, kind_above = kinds
    first_col, last_col, first_row, last_row = edges
    left_raw, right_raw, below_raw, above_raw = raw
    left_side = jnp.where(
        first_col,
        inflow_part,
        jnp.where(kind_left == 1, wall_density[0][..., None] * wall_shape, left_raw),
    )
    right_side = jnp.where(
        last_col,
        planes[2],
        jnp.where(kind_right == 1, wall_density[1][..., None] * wall_shape, right_raw),
    )
    below_side = jnp.where(
        first_row,
        planes[:, 0],
        jnp.where(kind_below == 1, wall_density[2][..., None] * wall_shape, below_raw),
    )
    above_side = jnp.where(
        last_row,
        planes[:, 2],
        jnp.where(kind_above == 1, wall_density[3][..., None] * wall_shape, above_raw),
    )
    particle_crowding = node_fields[0][..., None]
    mean_flow_first_axis = node_fields[1][..., None]
    mean_flow_second_axis = node_fields[2][..., None]
    mean_flow_third_axis = node_fields[3][..., None]
    kinetic_heat_level = node_fields[4][..., None]
    heat_variance = (
        (speed_x - mean_flow_first_axis) ** 2
        + (speed_y - mean_flow_second_axis) ** 2
        + (speed_z - mean_flow_third_axis) ** 2
    )
    gaussian_target_state = (
        particle_crowding
        / (kinetic_heat_level * jnp.sqrt(kinetic_heat_level))
        * jnp.exp(-heat_variance / (2.0 * kinetic_heat_level))
    )
    bgk_decay_update = particle_crowding * jnp.sqrt(kinetic_heat_level) / rarefaction_ratio
    update = -2.0 * (
        speed_x * derivative(planes, 0) + speed_y * derivative(planes, 1)
    ) + bgk_decay_update * (gaussian_target_state - planes)
    update = update.at[0].add(6.0 * jnp.maximum(speed_x, 0.0) * (left_side - planes[0]))
    update = update.at[2].add(6.0 * jnp.maximum(-speed_x, 0.0) * (right_side - planes[2]))
    update = update.at[:, 0].add(6.0 * jnp.maximum(speed_y, 0.0) * (below_side - planes[:, 0]))
    update = update.at[:, 2].add(6.0 * jnp.maximum(-speed_y, 0.0) * (above_side - planes[:, 2]))
    return jnp.where(own_kind == 1, planes, planes + time_step * update)


def shards(dist, cell_kind, inflow):
    count = dist.shape[4]
    width_x = dist.shape[2]
    width_y = dist.shape[3]
    index = lax.axis_index("vel") * count + jnp.arange(count, dtype=jnp.int32)
    totals = jnp.dot(
        dist.reshape(-1, count),
        moment_rows(index).T,
        precision=lax.Precision.HIGHEST,
        preferred_element_type=jnp.float32,
    )
    fluid_averages, exit_edge_condition = split_sums(totals.T.reshape(9, 3, 3, width_x, width_y))
    heat_speed_factor = wall_scale()
    summed = lax.psum((fluid_averages, exit_edge_condition), "vel")
    node_fields, wall_density = parameters(summed[0], summed[1], heat_speed_factor)
    padded = extended(dist, (("gx", 2), ("gy", 3)), 1)
    left_raw = padded[2, :, :width_x, 1:-1]
    right_raw = padded[0, :, 2:, 1:-1]
    below_raw = padded[:, 2, 1:-1, :width_y]
    above_raw = padded[:, 0, 1:-1, 2:]
    start_x = lax.axis_index("gx") * width_x
    start_y = lax.axis_index("gy") * width_y
    kinds = neighbor_kinds(cell_kind, start_x, start_y, width_x, width_y)
    edges = edge_masks(
        start_x,
        start_y,
        width_x,
        width_y,
        width_x * lax.axis_size("gx"),
        width_y * lax.axis_size("gy"),
    )
    fresh = section(
        dist,
        index,
        inflow,
        node_fields,
        wall_density,
        kinds,
        edges,
        (left_raw, right_raw, below_raw, above_raw),
    )
    return (fresh, node_fields)


def solution(mesh):
    in_specs = (P(None, None, "gx", "gy", "vel"), P(), P("vel"))
    out_specs = (P(None, None, "gx", "gy", "vel"), P(None, None, None, "gx", "gy"))
    return jax.shard_map(shards, mesh=mesh, in_specs=in_specs, out_specs=out_specs, check_vma=False)
```

profile of v0, /device:TPU:8, one launch (start us, length us, event | category | flops | bytes accessed | tf_op | source)
XLA Modules:
  0.0 236.4 jit_solution(10614652996879183584)
XLA Ops:
  7.4 6.2 %fusion.62 = f32[9,4608]{1,0:T(8,128)S(1)} fusion(f32[4608,256]{1,0:T(8,128)} %bitcast.43, f32[9,256]{1,0:T(8,128)S(1)} %stack.6), kind=kOutput, calls=%fused_computation.124 | convolution fusion | flops 127404288 | bytes 4893696 | tf_op jit(solution)/shard_map/dot_general | solution.py:197
  14.5 1.9 fusion.91
  16.5 1.9 collective-permute-start
  18.4 3.6 %collective-permute-start.1 = (f32[3,3,1,32,256]{4,3,2,1,0:T(8,128)}, f32[3,3,1,32,256]{4,3,2,1,0:T(8,128)}, u32[]{:S(2)}, u32[]{:S(2)}) collective-permute-start(f32[3,3,1,32,256]{4,3,2,1,0:T(8,128)} %get-tuple-element.65), channel_id=1, source_target_pairs={{2,0},{4,2},{6,4},{8,6},{10,8},{12,10},{14,12},{3,1},{5,3},{7,5},{... | collective-permute-start | bytes 884744 | tf_op jit(solution)/shard_map/ppermute | solution.py:24
  22.7 5.1 %copy.63 = f32[3,3,16,32,256]{4,2,3,1,0:T(8,128)S(1)} copy(f32[3,3,16,32,256]{4,3,2,1,0:T(8,128)} %param.11) | data formatting | bytes 9437184 | tf_op args[0]
  27.8 2.4 %multiply_subtract_fusion = (f32[3,1,16,32,256]{4,2,3,1,0:T(8,128)S(1)}, f32[3,1,16,32,256]{4,2,3,1,0:T(8,128)S(1)}, f32[3,1,16,32,256]{4,2,3,1,0:T(8,128)}) fusion(f32[3,3,16,32,256]{4,2,3,1,0:T(8,128)S(1)} %copy.63), kind=kLoop, calls=%fused_computation.39 | loop fusion | flops 4325376 | bytes 9437184 | tf_op jit(solution)/shard_map/sub | solution.py:109
  30.6 2.8 %multiply_subtract_fusion.1 = (f32[1,3,16,32,256]{4,2,3,1,0:T(8,128)}, f32[1,3,16,32,256]{4,2,3,1,0:T(8,128)}, f32[1,3,16,32,256]{4,2,3,1,0:T(8,128)}) fusion(f32[3,3,16,32,256]{4,2,3,1,0:T(8,128)S(1)} %copy.63), kind=kLoop, calls=%fused_computation.42 | loop fusion | flops 4325376 | bytes 9437184 | tf_op jit(solution)/shard_map/sub | solution.py:109
  36.9 82.1 %psum.15 = f32[4,3,16,32]{3,2,1,0:T(8,128)S(1)} all-reduce(f32[4,3,16,32]{3,2,1,0:T(8,128)S(1)} %pad_maximum_fusion.11), channel_id=1, replica_groups=mesh['vel'=16,'gx'=8,'gy'=2] {'vel'}, use_global_device_ids=true, to_apply=%region_1.2 | all-reduce | flops 6144 | bytes 49152 | tf_op jit(solution)/shard_map/psum | solution.py:205
  123.2 55.2 %all-reduce.3.cloned.1.call-done = f32[5,3,3,16,32]{4,3,2,1,0:T(8,128)} async-done(((f32[5,3,3,16,32]{4,3,2,1,0:T(8,128)}), f32[5,3,3,16,32]{4,3,2,1,0:T(8,128)}) %all-reduce.3.cloned.1.call-update) | async-done | bytes 92176 | tf_op jit(solution)/shard_map/psum | solution.py:205
  178.4 1.7 fusion.21
  180.2 1.5 fusion.22
  182.8 1.7 copy.43
  184.5 1.7 copy.45
  186.1 1.6 copy.46
  188.6 9.3 %fusion.2 = f32[3,3,16,32,256]{4,2,3,1,0:T(8,128)S(1)} fusion(f32[1,3,16,32,256]{4,2,3,1,0:T(8,128)} %get-tuple-element.72, f32[1,3,16,32,256]{4,2,3,1,0:T(8,128)} %get-tuple-element.71, f32[1,3,16,32,256]{4,2,3,1,0:T(8,128)} %get-tuple-element.70, f32[3,1,16,32,256]{4,2,3,1,0:T(8,128)} %get-tuple-element.69, ...), kind=kLoop, calls=%fused_computation.4 | loop fusion | flops 25952256 | bytes 18988032 | tf_op jit(solution)/shard_map/add | solution.py:182
  198.1 1.4 copy.52
  199.5 1.3 copy.56
  200.9 6.4 %collective-permute-start.2 = (f32[3,3,18,1,256]{4,2,3,1,0:T(8,128)S(1)}, f32[3,3,18,1,256]{4,2,3,1,0:T(8,128)S(1)}, u32[]{:S(2)}, u32[]{:S(2)}) collective-permute-start(f32[3,3,18,1,256]{4,2,3,1,0:T(8,128)S(1)} %get-tuple-element.64), channel_id=1, source_target_pairs={{0,1},{2,3},{4,5},{6,7},{8,9},{10,11},{12,13},{14,15},{16,17},{18,... | collective-permute-start | bytes 497672 | tf_op jit(solution)/shard_map/ppermute | solution.py:21
  207.3 1.5 collective-permute-start.3
  210.8 1.3 collective-permute-done.2
  212.1 1.2 fusion.8
  213.3 5.8 %collective-permute-done.3 = f32[3,3,18,1,256]{4,2,3,1,0:T(8,128)S(1)} collective-permute-done((f32[3,3,18,1,256]{4,2,3,1,0:T(8,128)S(1)}, f32[3,3,18,1,256]{4,2,3,1,0:T(8,128)S(1)}, u32[]{:S(2)}, u32[]{:S(2)}) %collective-permute-start.3) | collective-permute-done | bytes 165920 | tf_op jit(solution)/shard_map/ppermute | solution.py:24
  220.3 4.4 %add_select_fusion = f32[3,3,16,32,256]{4,2,3,1,0:T(8,128)S(1)} fusion(f32[3,3,16,32,256]{4,2,3,1,0:T(8,128)S(1)} %fusion.11, pred[16,32]{0,1:T(8,128)(4,1)S(1)} %get-tuple-element.79, f32[3,3,16,32,256]{4,3,2,1,0:T(8,128)S(1)} %bitcast.45), kind=kLoop, calls=%fused_computation | loop fusion | flops 3538944 | bytes 14156288 | tf_op jit(solution)/shard_map/jit(_where)/select_n | solution.py:189
  224.7 4.9 %copy.64 = f32[3,3,16,32,256]{4,3,2,1,0:T(8,128)} copy(f32[3,3,16,32,256]{4,2,3,1,0:T(8,128)S(1)} %add_select_fusion) | data formatting | bytes 9437184
  (90 shorter events, 14.8 us)
Async XLA Ops:
  7.2 171.3 %all-reduce.3.cloned.1.call-start = ((), (), s32[]{:S(2)}) async-start(), calls=%async_computation | async-start | bytes 737280 | tf_op jit(solution)/shard_map/psum | solution.py:205
  16.5 181.6 %collective-permute-start = (f32[3,3,1,32,256]{4,3,2,1,0:T(8,128)}, f32[3,3,1,32,256]{4,3,2,1,0:T(8,128)}, u32[]{:S(2)}, u32[]{:S(2)}) collective-permute-start(f32[3,3,1,32,256]{4,3,2,1,0:T(8,128)} %get-tuple-element.66), channel_id=1, source_target_pairs={{0,2},{2,4},{4,6},{6,8},{8,10},{10,12},{12,14},{1,3},{3,5},{5,7},{... | collective-permute-start | bytes 884744 | tf_op jit(solution)/shard_map/ppermute | solution.py:21
  18.4 181.1 %collective-permute-start.1 = (f32[3,3,1,32,256]{4,3,2,1,0:T(8,128)}, f32[3,3,1,32,256]{4,3,2,1,0:T(8,128)}, u32[]{:S(2)}, u32[]{:S(2)}) collective-permute-start(f32[3,3,1,32,256]{4,3,2,1,0:T(8,128)} %get-tuple-element.65), channel_id=1, source_target_pairs={{2,0},{4,2},{6,4},{8,6},{10,8},{12,10},{14,12},{3,1},{5,3},{7,5},{... | collective-permute-start | bytes 884744 | tf_op jit(solution)/shard_map/ppermute | solution.py:24
  27.8 2.8 %copy-start = (f32[3,3,16,32,256]{4,2,3,1,0:T(8,128)}, f32[3,3,16,32,256]{4,2,3,1,0:T(8,128)S(1)}, u32[]{:S(2)}) copy-start(f32[3,3,16,32,256]{4,2,3,1,0:T(8,128)S(1)} %copy.63) | copy-start | bytes 14155780
  33.4 89.0 %copy-start.6 = (s32[128,64]{0,1:T(8,128)S(1)}, s32[128,64]{0,1:T(8,128)}, u32[]{:S(2)}) copy-start(s32[128,64]{0,1:T(8,128)} %param.12) | copy-start | bytes 98308
  188.5 12.2 %slice-start = ((s8[4718592]{0:T(1024)(128)(4,1)}), s8[4194304]{0:T(1024)(128)(4,1)S(1)}, s32[]{:S(2)}) async-start(s8[4718592]{0:T(1024)(128)(4,1)} %bitcast.41), calls=%async_computation.1 | async-start | bytes 8388608
  188.5 9.4 %copy-start.1 = (f32[5,3,3,16,32]{4,3,2,1,0:T(8,128)S(1)}, f32[5,3,3,16,32]{4,3,2,1,0:T(8,128)}, u32[]{:S(2)}) copy-start(f32[5,3,3,16,32]{4,3,2,1,0:T(8,128)} %all-reduce.3.cloned.1.call-done) | copy-start | bytes 276484
  188.5 12.2 %slice-start.1 = ((s8[4718592]{0:T(1024)(128)(4,1)}), s8[524288]{0:T(1024)(128)(4,1)S(1)}, s32[]{:S(2)}) async-start(s8[4718592]{0:T(1024)(128)(4,1)} %bitcast.41), calls=%async_computation.2 | async-start | bytes 1048576
  198.1 2.9 %copy-start.7 = (f32[5,3,3,16,32]{4,3,2,1,0:T(8,128)}, f32[5,3,3,16,32]{4,3,2,1,0:T(8,128)S(1)}, u32[]{:S(2)}) copy-start(f32[5,3,3,16,32]{4,3,2,1,0:T(8,128)S(1)} %multiply_dynamic-update-slice_fusion) | copy-start | bytes 276484
  200.8 8.0 %copy-start.3 = (f32[3,16,32]{1,2,0:T(8,128)S(1)}, f32[3,16,32]{1,2,0:T(8,128)}, u32[]{:S(2)}) copy-start(f32[3,16,32]{1,2,0:T(8,128)} %copy.51) | copy-start | bytes 18436
  200.8 8.0 %copy-start.9 = (f32[256]{0:T(256)S(1)}, f32[256]{0:T(256)}, u32[]{:S(2)}) copy-start(f32[256]{0:T(256)} %param.13) | copy-start | bytes 3076
  200.8 8.0 %copy-start.10 = (f32[256]{0:T(256)S(1)}, f32[256]{0:T(256)}, u32[]{:S(2)}) copy-start(f32[256]{0:T(256)} %maximum_multiply_fusion.5) | copy-start | bytes 3076
  200.8 8.0 %copy-start.13 = (pred[16]{0:T(512)(128)(4,1)S(1)}, pred[16]{0:T(512)(128)(4,1)}, u32[]{:S(2)}) copy-start(pred[16]{0:T(512)(128)(4,1)} %fusion.88) | copy-start | bytes 52
  200.9 11.1 %collective-permute-start.2 = (f32[3,3,18,1,256]{4,2,3,1,0:T(8,128)S(1)}, f32[3,3,18,1,256]{4,2,3,1,0:T(8,128)S(1)}, u32[]{:S(2)}, u32[]{:S(2)}) collective-permute-start(f32[3,3,18,1,256]{4,2,3,1,0:T(8,128)S(1)} %get-tuple-element.64), channel_id=1, source_target_pairs={{0,1},{2,3},{4,5},{6,7},{8,9},{10,11},{12,13},{14,15},{16,17},{18,... | collective-permute-start | bytes 497672 | tf_op jit(solution)/shard_map/ppermute | solution.py:21
  207.3 11.7 %collective-permute-start.3 = (f32[3,3,18,1,256]{4,2,3,1,0:T(8,128)S(1)}, f32[3,3,18,1,256]{4,2,3,1,0:T(8,128)S(1)}, u32[]{:S(2)}, u32[]{:S(2)}) collective-permute-start(f32[3,3,18,1,256]{4,2,3,1,0:T(8,128)S(1)} %get-tuple-element.63), channel_id=1, source_target_pairs={{1,0},{3,2},{5,4},{7,6},{9,8},{11,10},{13,12},{15,14},{17,16},{19,... | collective-permute-start | bytes 497672 | tf_op jit(solution)/shard_map/ppermute | solution.py:24
  208.9 0.9 copy-start.5
  208.9 0.9 copy-start.8
  208.9 0.9 copy-start.14
  209.8 2.3 copy-start.4
  209.8 2.3 copy-start.12
  212.1 7.0 %copy-start.2 = (f32[3,16,32]{1,2,0:T(8,128)S(1)}, f32[3,16,32]{1,2,0:T(8,128)}, u32[]{:S(2)}) copy-start(f32[3,16,32]{1,2,0:T(8,128)} %copy.61) | copy-start | bytes 18436
  212.1 7.0 %copy-start.11 = (pred[32]{0:T(512)(128)(4,1)S(1)}, pred[32]{0:T(512)(128)(4,1)}, u32[]{:S(2)}) copy-start(pred[32]{0:T(512)(128)(4,1)} %get-tuple-element.96) | copy-start | bytes 100
  212.1 8.2 %slice-start.2 = ((s8[4718592]{0:T(1024)(128)(4,1)}), s8[4194304]{0:T(1024)(128)(4,1)S(1)}, s32[]{:S(2)}) async-start(s8[4718592]{0:T(1024)(128)(4,1)} %bitcast.44), calls=%async_computation.3 | async-start | bytes 8388608
  219.1 1.2 slice-start.3
Sparse Core Ops, SparseCore 0:
  14.7 163.7 all-reduce.2
where the time goes:
time: 237 us; the launch traced here: 236 us
  blocking collectives  82.1 us (35%)
  waiting for transfers between devices  62.3 us (26%)
  other arithmetic  31.6 us (13%)
  local copies, waits for them, and re-layouts  26.1 us (11%)
  between operations  14.5 us (6%)
  starting transfers between devices  13.5 us (6%)
  matrix products  6.22 us (3%)
    psum x1, blocking collectives, shards(): summed = lax.psum((fluid_averages, exit_edge_condition), 'vel')  82.1 us
    psum x1, waiting for transfers between devices, shards(): summed = lax.psum((fluid_averages, exit_edge_condition), 'vel')  55.2 us
    unnamed x41, local copies, waits for them, and re-layouts  10.5 us
    add x1, other arithmetic, section(): -2.0 * (speed_x * derivative(planes, 0) + speed_y * derivative(planes, 1))  9.34 us
    ppermute x2, starting transfers between devices, extended(): lax.ppermute(lax.slice_in_dim(block, block.shape[dim] - width, None, axis...  8.32 us
    dot_general x1, matrix products, shards(): jnp.dot(dist.reshape(-1, count), moment_rows(index).T, precision=lax.Prec...  6.22 us
    ppermute x2, waiting for transfers between devices, extended(): lax.ppermute(lax.slice_in_dim(block, 0, width, axis=dim), axis, backward)  5.79 us
    sub x2, other arithmetic, derivative(): -1.5 * first + 2.0 * middle - 0.5 * final  5.21 us
  transfers between devices with their start and end apart: 5, of which 3 were waited for; matrix products, arithmetic and copies ran while one was open for 19% of the time, Pallas kernels for 0%

commit v1 on v0

v1 whole, which is shorter than its diff:
```python
import math

import jax
import jax.numpy as jnp
import ml_dtypes
import numpy as np
from jax import lax
from jax.experimental import pallas as pl
from jax.experimental.pallas import tpu as pltpu
from jax.sharding import PartitionSpec as P

NV = 16
SPACING = 10.0 / NV
VEL_MAX = 5.0
RAREFACTION = 0.25
TIME_STEP = 0.08
WEIGHT = SPACING**3 / (2.0 * math.pi) ** 1.5

LANES = NV * NV
HALF = LANES // 2
SUM_ROWS = 208
TAIL = 160
COEF_ROWS = 32
MASK_ROWS = 16
CHUNKS = 4
F32 = jnp.float32
BF16 = jnp.bfloat16


def levels():
    return (np.arange(NV) + 0.5) * SPACING - VEL_MAX


def lane_speeds():
    return np.repeat(levels(), NV), np.tile(levels(), NV)


def wall_scale():
    level = levels()
    gauss = np.exp(-0.5 * level * level)
    return float(WEIGHT * np.sum(np.maximum(-level, 0.0) * gauss) * np.sum(gauss) ** 2)


def pieces(value, count):
    out = []
    for _ in range(count):
        piece = value.astype(ml_dtypes.bfloat16).astype(np.float64)
        out.append(piece)
        value = value - piece
    return out


def spread_weights():
    vy, vz = lane_speeds()
    square = vy * vy + vz * vz
    wall = np.exp(-0.5 * square)
    table = np.zeros((COEF_ROWS, 2 * LANES + HALF))
    high, low = pieces(square, 2)
    for row in range(3):
        table[row, :LANES] = 1.0
        table[3 + row, :LANES] = vy
        table[6 + row, :LANES] = vz
        table[9 + row, :LANES] = high
        table[12 + row, :LANES] = low
    table[15:17, 2 * LANES :] = 1.0
    for base, shape in (
        (17, wall),
        (20, np.maximum(vy, 0.0) * wall),
        (23, np.maximum(-vy, 0.0) * wall),
    ):
        first, second = pieces(shape, 2)
        table[base, LANES : 2 * LANES] = first
        table[base + 1, LANES : 2 * LANES] = second
        table[base + 2, LANES : 2 * LANES] = first
    return jnp.asarray(table.astype(ml_dtypes.bfloat16))


def own_speed():
    level = lax.axis_index("vel")
    return level, (level.astype(F32) + 0.5) * SPACING - VEL_MAX


def lane_axis(shape, axis):
    return lax.broadcasted_iota(jnp.int32, shape, axis)


def moment_weights():
    row = lane_axis((16, LANES), 0)
    lane = lane_axis((16, LANES), 1)
    vy = ((lane // NV).astype(F32) + 0.5) * SPACING - VEL_MAX
    vz = ((lane % NV).astype(F32) + 0.5) * SPACING - VEL_MAX
    square = vy * vy + vz * vz
    high = square.astype(BF16).astype(F32)
    table = jnp.zeros((16, LANES), F32)
    for at, value in enumerate(
        (1.0, vy, vz, high, square - high, jnp.maximum(-vy, 0.0), jnp.maximum(vy, 0.0))
    ):
        table = jnp.where(row == at, value, table)
    return table.astype(BF16)


def kind_masks(kinds, masks, wx, wy, forward):
    n = wx * wy
    size_y, size_x = kinds.shape
    start_x = lax.axis_index("gx") * wx
    start_y = lax.axis_index("gy") * wy
    behind = jnp.where(forward, 1, -1)
    kind = kinds[...].astype(F32).astype(BF16)
    x = lane_axis((size_x, n), 0)
    own_x = start_x + lane_axis((size_x, n), 1) // wy
    y = lane_axis((size_y, n), 0)
    own_y = start_y + lane_axis((size_y, n), 1) % wy

    def pick(column):
        chosen = jnp.where(x == column, 1.0, 0.0).astype(BF16)
        return jnp.dot(kind, chosen, preferred_element_type=F32)

    def at(table, row):
        return jnp.sum(jnp.where(y == row, table, 0.0), axis=0, keepdims=True)

    here = pick(own_x)
    fluid = 1.0 - at(here, own_y)
    solid_x = at(pick(own_x - behind), own_y)
    solid_b = at(here, own_y - 1)
    solid_a = at(here, own_y + 1)
    column, row = own_x[0:1], own_y[0:1]
    last_x = jnp.logical_and(jnp.logical_not(forward), column == size_x - 1)
    inner_x = jnp.where(last_x, 0.0, fluid)
    inner_b = jnp.where(row == 0, 0.0, fluid)
    inner_a = jnp.where(row == size_y - 1, 0.0, fluid)
    masks[...] = jnp.zeros_like(masks)
    for at_row, value in enumerate(
        (
            fluid,
            inner_x * (1.0 - solid_x),
            inner_x,
            inner_b * (1.0 - solid_b),
            inner_b,
            inner_a * (1.0 - solid_a),
            inner_a,
            fluid * solid_x,
            fluid * solid_b,
            fluid * solid_a,
        )
    ):
        masks[at_row : at_row + 1, :] = value


def moments_kernel(wx, wy, dist, kinds, sums, face_x, face_y, masks, dv, kind, sems):
    n = wx * wy
    copies = [pltpu.make_async_copy(dist.at[k], dv.at[k], sems.at[k]) for k in range(9)]
    kind_copy = pltpu.make_async_copy(kinds, kind, sems.at[9])
    copies[0].start()
    kind_copy.start()
    for copy in copies[1:]:
        copy.start()
    level, vx = own_speed()
    sums[...] = jnp.zeros_like(sums)
    table = moment_weights()
    kind_copy.wait()
    kind_masks(kind, masks, wx, wy, level >= NV // 2)
    forward = level >= NV // 2
    contract = (((1,), (1,)), ((), ()))

    def put(first, step, row):
        for c in range(n // HALF):
            at = first + c * step
            sums[at : at + 1, :] = row[:, c * HALF : (c + 1) * HALF]

    walls_x, walls_y = [None] * 3, [None] * 3
    for k in range(9):
        i, j = divmod(k, 3)
        copies[k].wait()
        plane = dv[k]
        high = plane.astype(BF16)
        low = (plane - high.astype(F32)).astype(BF16)
        part = lax.dot_general(table, high, contract, preferred_element_type=F32)
        part = part + lax.dot_general(table, low, contract, preferred_element_type=F32)
        part = part * WEIGHT
        total = part[0:1]
        rows = (
            total,
            vx * total,
            part[1:2],
            part[2:3],
            0.5 * (vx * vx * total + part[3:4] + part[4:5]),
        )
        for f, row in enumerate(rows):
            if k < 8:
                put(f * 32 + k, 8, row)
            else:
                put(TAIL + f * 4, 1, row)
        if i == 0:
            walls_x[j] = total
        if i == 2:
            put(TAIL + (5 + j) * 4, 1, jnp.abs(vx) * jnp.where(forward, total, walls_x[j]))
        if j == 0:
            walls_y[i] = part[5:6] * masks[8:9, :]
        if j == 2:
            put(TAIL + (8 + i) * 4, 1, walls_y[i] + part[6:7] * masks[9:10, :])

    @pl.when(level >= NV // 2)
    def _():
        for j in range(3):
            face_x[j] = dv[6 + j, n - wy : n, :]

    @pl.when(level < NV // 2)
    def _():
        for j in range(3):
            face_x[j] = dv[j, 0:wy, :]

    @pl.when(lax.axis_index("gy") == 0)
    def _():
        for i in range(3):
            for p in range(wx):
                at = p * wy + wy - 1
                face_y[i, p : p + 1, :] = dv[3 * i + 2, at : at + 1, HALF:]

    @pl.when(lax.axis_index("gy") != 0)
    def _():
        for i in range(3):
            for p in range(wx):
                at = p * wy
                face_y[i, p : p + 1, :] = dv[3 * i, at : at + 1, :HALF]


def advect_kernel(wx, wy, dist, table, masks, out, dv, edge_x, edge_y, weights, spread, sems):
    level, vx = own_speed()
    keep = pltpu.make_async_copy(table, weights, sems.at[CHUNKS])
    keep.start()
    row = lane_axis((MASK_ROWS, 7 * HALF), 0)
    column = lane_axis((MASK_ROWS, 7 * HALF), 1)
    select = jnp.where(column // HALF == row, 1.0, 0.0).astype(BF16)
    cx = -TIME_STEP * vx
    face_cx = 6.0 * TIME_STEP * jnp.abs(vx)
    lane = lane_axis((1, HALF), 1)
    q = lane_axis((wy, HALF), 0)

    def speed_y(half):
        return ((lane // NV + half * (NV // 2)).astype(F32) + 0.5) * SPACING - VEL_MAX

    def differences(a):
        four = 4.0 * a[1]
        rest = four - (a[0] + a[2])
        return rest - 2.0 * a[0], a[2] - a[0], 2.0 * a[2] - rest

    def tile(p, half, sign, trace):
        rows = pl.ds(pl.multiple_of(p * wy, wy), wy)
        lanes = slice(half * HALF, (half + 1) * HALF)
        vy = speed_y(half)
        cy = -TIME_STEP * vy
        face_cy = 6.0 * TIME_STEP * jnp.abs(vy)
        d = [[dv[3 * i + j, rows, lanes] for j in range(3)] for i in range(3)]
        fluid, wall_x, own_x, wall_b, own_b, wall_a, own_a = [
            spread[rows, m * HALF : (m + 1) * HALF] for m in range(7)
        ]
        dx = [differences([d[i][j] for i in range(3)]) for j in range(3)]
        for i in range(3):
            dy = differences(d[i])
            for j in range(3):
                value = d[i][j] + fluid * (cx * dx[j][i] + cy * dy[j])
                if i == (0 if sign > 0 else 2):
                    change = own_x * d[i][j]
                    if trace is not None:
                        change = change - wall_x * trace(j, lanes)
                    value = value - face_cx * change
                if half == 1 and j == 0:
                    raw = jnp.where(q == 0, 0.0, pltpu.roll(d[i][2], 1, 0))
                    value = value + face_cy * (wall_b * raw - own_b * d[i][j])
                if half == 0 and j == 2:
                    raw = jnp.where(q == wy - 1, 0.0, pltpu.roll(d[i][0], wy - 1, 0))
                    value = value + face_cy * (wall_a * raw - own_a * d[i][j])
                out[3 * i + j, rows, lanes] = value

    def sweep(sign):
        edge = 0 if sign > 0 else wx - 1
        source = 6 if sign > 0 else 0
        share = wx // CHUNKS
        order = range(CHUNKS) if sign > 0 else range(CHUNKS)[::-1]

        def part(chunk):
            rows = slice(chunk * share * wy, (chunk + 1) * share * wy)
            return pltpu.make_async_copy(dist.at[:, rows], dv.at[:, rows], sems.at[chunk])

        for chunk in order:
            part(chunk).start()
        spread[...] = lax.dot_general(
            masks[...].astype(BF16), select, (((0,), (0,)), ((), ())), preferred_element_type=F32
        )
        edge_x[...] = face_cx * spread[edge * wy : (edge + 1) * wy, HALF : 2 * HALF]
        for chunk in order:
            part(chunk).wait()
            low, high = chunk * share, (chunk + 1) * share
            if chunk == order[0]:
                for half in range(2):
                    tile(edge, half, sign, None)
                low, high = (low + 1, high) if sign > 0 else (low, high - 1)

            @pl.loop(low, high)
            def _(p):
                behind = pl.ds(pl.multiple_of((p - sign) * wy, wy), wy)
                for half in range(2):
                    tile(p, half, sign, lambda j, lanes: dv[source + j, behind, lanes])

    @pl.when(level >= NV // 2)
    def _():
        sweep(1)

    @pl.when(level < NV // 2)
    def _():
        sweep(-1)

    upper = lax.axis_index("gy") != 0

    @pl.when(upper)
    def _():
        for p in range(wx):
            at = p * wy
            edge_y[p : p + 1, :] = spread[at : at + 1, 3 * HALF : 4 * HALF] * (
                6.0 * TIME_STEP * speed_y(1)
            )

    @pl.when(jnp.logical_not(upper))
    def _():
        for p in range(wx):
            at = p * wy + wy - 1
            edge_y[p : p + 1, :] = spread[at : at + 1, 5 * HALF : 6 * HALF] * (
                -6.0 * TIME_STEP * speed_y(0)
            )

    keep.wait()


def edges_kernel(wx, wy, inside, halo_x, halo_y, inflow, edge_x, edge_y, out):
    del inside
    level, _ = own_speed()
    forward = level >= NV // 2
    upper = lax.axis_index("gy") != 0
    first_x = lax.axis_index("gx") == 0

    def along_x(p, i, outside):
        rows = slice(p * wy, (p + 1) * wy)
        for j in range(3):
            for half in range(2):
                lanes = slice(half * HALF, (half + 1) * HALF)
                out[3 * i + j, rows, lanes] += edge_x[...] * outside(j, lanes)

    def along_y(q, j, lanes):
        for i in range(3):
            for p in range(wx):
                at = slice(p * wy + q, p * wy + q + 1)
                out[3 * i + j, at, lanes] += edge_y[p : p + 1, :] * halo_y[i, p : p + 1, :]

    @pl.when(forward)
    def _():
        along_x(0, 0, lambda j, at: jnp.where(first_x, inflow[:, at], halo_x[j, :, at]))

    @pl.when(jnp.logical_not(forward))
    def _():
        along_x(wx - 1, 2, lambda j, at: halo_x[j, :, at])

    @pl.when(upper)
    def _():
        along_y(0, 0, slice(HALF, LANES))

    @pl.when(jnp.logical_not(upper))
    def _():
        along_y(wy - 1, 2, slice(0, HALF))


def split(value, count):
    out = []
    for _ in range(count):
        piece = value.astype(BF16).astype(F32)
        out.append(piece)
        value = value - piece
    return out


def relax_kernel(
    wx,
    wy,
    sums_a,
    sums_b,
    masks,
    table,
    advected,
    dv,
    out,
    fields_out,
    coef,
    fields,
    result,
    sems,
):
    n = wx * wy
    level, vx = own_speed()
    is_forward = level >= NV // 2
    parts = range(n // HALF)

    def wide(read, first, step, count):
        return jnp.concatenate(
            [read(slice(first + c * step, first + c * step + count)) for c in parts], axis=1
        )

    def both(rows):
        return sums_a[rows, :] + sums_b[rows, :]

    def received(rows):
        return sums_b[rows, :]

    fluid = masks[0:1, :]
    coef[...] = jnp.zeros_like(coef)
    log2e = math.log2(math.e)

    def store(planes, start, value, count):
        for piece_at, piece in enumerate(split(value, count)):
            coef[planes, start + piece_at, :] = piece

    for planes, where, s in (
        (slice(0, 8), 0, [wide(both, f * 32, 8, 8) for f in range(5)]),
        (slice(8, 9), 8, [wide(both, TAIL + f * 4, 1, 1) for f in range(5)]),
    ):
        rho = s[0]
        ux, uy, uz = s[1] / rho, s[2] / rho, s[3] / rho
        temp = 2.0 / 3.0 * (s[4] / rho - 0.5 * (ux * ux + uy * uy + uz * uz))
        for f, value in enumerate((rho, ux, uy, uz, temp)):
            at = f * 9 + where
            fields[at : at + value.shape[0], :] = value
        rate = rho * jnp.sqrt(temp) / RAREFACTION * TIME_STEP * fluid
        slope = (0.5 * log2e) / temp
        height = (
            2.0 * jnp.log2(rho)
            - jnp.log2(temp)
            + math.log2(TIME_STEP / RAREFACTION)
            - slope * ((vx - ux) * (vx - ux) + uy * uy + uz * uz)
        )
        height = jnp.where(fluid == 0.0, -1e30, height)
        store(planes, 0, height, 3)
        store(planes, 3, 2.0 * slope * uy, 3)
        store(planes, 6, 2.0 * slope * uz, 3)
        store(planes, 9, -slope, 3)
        store(planes, 12, -slope, 3)
        store(planes, 15, rate, 2)

    def store_wall(k, start, value):
        first, second = split(value, 2)
        coef[k, start : start + 1, :] = first
        coef[k, start + 1 : start + 2, :] = first
        coef[k, start + 2 : start + 3, :] = second

    scale = 6.0 * TIME_STEP / wall_scale()
    forward = is_forward.astype(F32)
    gauss_x = jnp.exp(jnp.full((1, n), -0.5, F32) * (vx * vx)) * scale
    solid_x = masks[7:8, :] * gauss_x * jnp.abs(vx)
    solid_b = masks[8:9, :] * gauss_x
    solid_a = masks[9:10, :] * gauss_x
    for j in range(3):
        value = solid_x * wide(received, TAIL + (5 + j) * 4, 1, 1)
        store_wall(j, 17, value * forward)
        store_wall(6 + j, 17, value * (1.0 - forward))
    for i in range(3):
        value = wide(both, TAIL + (8 + i) * 4, 1, 1)
        store_wall(3 * i, 20, solid_b * value)
        store_wall(3 * i + 2, 23, solid_a * value)

    weights = table[...]
    chunk = min(256, n)
    copies = []
    for k in range(9):
        for start in range(0, n, chunk):
            rows = slice(start, start + chunk)
            spread = lax.dot_general(
                coef[k, :, rows].astype(BF16),
                weights,
                (((0,), (0,)), ((), ())),
                preferred_element_type=F32,
            )
            rate = spread[:, 2 * LANES :]
            for half in range(2):
                lanes = slice(half * HALF, (half + 1) * HALF)
                target = jnp.exp2(spread[:, lanes])
                wall = spread[:, LANES + half * HALF : LANES + (half + 1) * HALF]
                result[k, rows, lanes] = (
                    advected[k, rows, lanes] - rate * dv[k, rows, lanes] + (target + wall)
                )
        copy = pltpu.make_async_copy(result.at[k], out.at[k], sems.at[k])
        copy.start()
        copies.append(copy)
    for p in range(wx):
        fields_out[:, p, :] = fields[0:45, p * wy : (p + 1) * wy]
    for copy in copies:
        copy.wait()


def exchanges():
    count = lax.axis_size("vel")
    return (
        [(v, v ^ 1) for v in range(count)],
        [(v, v ^ 3) for v in range(count)],
        [(v, v ^ 4) for v in range(count)],
        [(v, v ^ 8) for v in range(count)],
    )


def upwind_pairs():
    count = lax.axis_size("gx")
    pairs = []
    for v in range(lax.axis_size("vel")):
        step = 1 if v >= NV // 2 else -1
        for g in range(count):
            if 0 <= g + step < count:
                pairs.append((v * count + g, v * count + g + step))
    return pairs


def vmem(shape):
    return pltpu.VMEM(shape, F32)


def in_vmem(x):
    return pltpu.with_memory_space_constraint(x, pltpu.VMEM)


def shards(dist, cell_kind, inflow):
    wx, wy = dist.shape[2], dist.shape[3]
    n = wx * wy
    whole = pl.BlockSpec(memory_space=pltpu.VMEM)
    anywhere = pl.BlockSpec(memory_space=pl.ANY)
    planes = pltpu.with_memory_space_constraint(dist.reshape(9, n, LANES), pltpu.HBM)
    sums, face_x, face_y, masks = pl.pallas_call(
        lambda *refs: moments_kernel(wx, wy, *refs),
        out_shape=(
            vmem((SUM_ROWS, HALF)),
            vmem((3, wy, LANES)),
            vmem((3, wx, HALF)),
            vmem((MASK_ROWS, n)),
        ),
        in_specs=[anywhere, anywhere],
        out_specs=(whole, whole, whole, whole),
        scratch_shapes=[
            pltpu.VMEM((9, n, LANES), F32),
            pltpu.VMEM(cell_kind.shape[::-1], jnp.int32),
            pltpu.SemaphoreType.DMA((10,)),
        ],
        compiler_params=pltpu.CompilerParams(vmem_limit_bytes=16 << 20),
        cost_estimate=pl.CostEstimate(
            flops=2 * 32 * 9 * n * LANES, bytes_accessed=4 * 9 * n * LANES, transcendentals=0
        ),
        name="moments",
    )(planes, pltpu.with_memory_space_constraint(cell_kind.T, pltpu.HBM))
    table = spread_weights()
    advected, held, edge_x, edge_y, table = pl.pallas_call(
        lambda *refs: advect_kernel(wx, wy, *refs),
        out_shape=(
            vmem((9, n, LANES)),
            vmem((9, n, LANES)),
            vmem((wy, HALF)),
            vmem((wx, HALF)),
            pltpu.VMEM(table.shape, table.dtype),
        ),
        in_specs=[anywhere, anywhere, whole],
        out_specs=(whole,) * 5,
        scratch_shapes=[pltpu.VMEM((n, 7 * HALF), F32), pltpu.SemaphoreType.DMA((CHUNKS + 1,))],
        compiler_params=pltpu.CompilerParams(vmem_limit_bytes=8 << 20),
        cost_estimate=pl.CostEstimate(
            flops=20 * 9 * n * LANES, bytes_accessed=12 * 9 * n * LANES, transcendentals=0
        ),
        name="advect",
    )(planes, pltpu.with_memory_space_constraint(table, pltpu.HBM), masks)
    steps = exchanges()
    total = sums + lax.ppermute(sums, "vel", steps[0])
    total = total + lax.ppermute(total, "vel", steps[1])
    total, edge_x, edge_y = lax.optimization_barrier((total, edge_x, edge_y))
    halo_x = lax.ppermute(face_x, ("vel", "gx"), upwind_pairs())
    total = total + lax.ppermute(total, "vel", steps[2])
    total, halo_x = lax.optimization_barrier((total, halo_x))
    other = lax.ppermute(total, "vel", steps[3])
    halo_y = lax.ppermute(face_y, "gy", [(0, 1), (1, 0)])
    advected = pl.pallas_call(
        lambda *refs: edges_kernel(wx, wy, *refs),
        out_shape=vmem((9, n, LANES)),
        in_specs=[whole] * 6,
        out_specs=whole,
        input_output_aliases={0: 0},
        compiler_params=pltpu.CompilerParams(vmem_limit_bytes=4 << 20),
        cost_estimate=pl.CostEstimate(
            flops=100 * 9 * n * LANES, bytes_accessed=40 * 9 * n * LANES, transcendentals=0
        ),
        name="edges",
    )(in_vmem(advected), halo_x, halo_y, inflow[None, :], edge_x, edge_y)
    fresh, fields = pl.pallas_call(
        lambda *refs: relax_kernel(wx, wy, *refs),
        out_shape=(
            jax.ShapeDtypeStruct((9, n, LANES), F32),
            jax.ShapeDtypeStruct((45, wx, wy), F32),
        ),
        in_specs=[whole] * 6,
        out_specs=(anywhere, whole),
        scratch_shapes=[
            pltpu.VMEM((9, COEF_ROWS, n), F32),
            pltpu.VMEM((48, n), F32),
            pltpu.VMEM((9, n, LANES), F32),
            pltpu.SemaphoreType.DMA((9,)),
        ],
        compiler_params=pltpu.CompilerParams(vmem_limit_bytes=16 << 20),
        name="relax",
    )(
        total,
        other,
        masks,
        table,
        in_vmem(advected),
        in_vmem(held),
    )
    return (fresh.reshape(dist.shape), fields.reshape(5, 3, 3, wx, wy))


def solution(mesh):
    in_specs = (P(None, None, "gx", "gy", "vel"), P(), P("vel"))
    out_specs = (P(None, None, "gx", "gy", "vel"), P(None, None, None, "gx", "gy"))
    return jax.shard_map(shards, mesh=mesh, in_specs=in_specs, out_specs=out_specs, check_vma=False)
```

time: 237 us -> 38.7 us (0.16)
  blocking collectives: 82.1 us -> 0 us
  waiting for transfers between devices: 62.3 us -> 8.64 us
  other arithmetic: 31.6 us -> 0.04 us
  local copies, waits for them, and re-layouts: 26.1 us -> 0.01 us
  between operations: 14.5 us -> 0.7 us
  Pallas kernels: 0 us -> 11.3 us
  matrix products: 6.22 us -> 0 us
  starting transfers between devices: 13.5 us -> 17.9 us
    psum x1 -> x0, blocking collectives: 82.1 us -> none  [shards(): summed = lax.psum((fluid_averages, exit_edge_condition), 'vel')]
    psum x1 -> x0, waiting for transfers between devices: 55.2 us -> none  [shards(): summed = lax.psum((fluid_averages, exit_edge_condition), 'vel')]
    pallas_call x0 -> x4, Pallas kernels: none -> 11.3 us  [the longest x1 3.87 us: shards(): pl.pallas_call(lambda *refs: relax_kernel(wx, wy, *refs), out_shape=(jax....]
    unnamed x41 -> x2, local copies, waits for them, and re-layouts: 10.5 us -> 0.01 us
    add x1 -> x3, other arithmetic: 9.34 us -> 0.04 us  [the longest x1 0.01 us: shards(): total = sums + lax.ppermute(sums, 'vel', steps[0])]
    dot_general x1 -> x0, matrix products: 6.22 us -> none  [shards(): jnp.dot(dist.reshape(-1, count), moment_rows(index).T, precision=lax.Prec...]
    sub x5 -> x0, other arithmetic: 5.87 us -> none  [the longest x2 5.21 us: derivative(): -1.5 * first + 2.0 * middle - 0.5 * final]
    div x5 -> x0, local copies, waits for them, and re-layouts: 5.84 us -> none  [the longest x1 1.66 us: section(): particle_crowding * jnp.sqrt(kinetic_heat_level) / rarefaction_ratio]
  transfers between devices with their start and end apart: 5 -> 6, of which waited for: 3 -> 4; matrix products, arithmetic and copies ran while one was open for 19% -> 0% of each run, Pallas kernels for 0% -> 10%
where the time goes in v1:
time: 38.7 us; the launch traced here: 38.6 us
  starting transfers between devices  17.9 us (46%)
  Pallas kernels  11.3 us (29%)
  waiting for transfers between devices  8.64 us (22%)
  between operations  0.7 us (2%)
    ppermute x1, starting transfers between devices, shards(): other = lax.ppermute(total, 'vel', steps[3])  5.09 us
    ppermute x1, starting transfers between devices, shards(): halo_y = lax.ppermute(face_y, 'gy', [(0, 1), (1, 0)])  4.49 us
    pallas_call x1, Pallas kernels, shards(): pl.pallas_call(lambda *refs: relax_kernel(wx, wy, *refs), out_shape=(jax....  3.87 us
    pallas_call x1, Pallas kernels, shards(): pl.pallas_call(lambda *refs: advect_kernel(wx, wy, *refs), out_shape=(vme...  3.7 us
    pallas_call x1, Pallas kernels, shards(): pl.pallas_call(lambda *refs: moments_kernel(wx, wy, *refs), out_shape=(vm...  3.64 us
    ppermute x1, waiting for transfers between devices, shards(): halo_y = lax.ppermute(face_y, 'gy', [(0, 1), (1, 0)])  3.24 us
    ppermute x1, waiting for transfers between devices, shards(): total = sums + lax.ppermute(sums, 'vel', steps[0])  3.22 us
    ppermute x1, starting transfers between devices, shards(): total = total + lax.ppermute(total, 'vel', steps[1])  2.85 us
  transfers between devices with their start and end apart: 6, of which 4 were waited for; matrix products, arithmetic and copies ran while one was open for 0% of the time, Pallas kernels for 10%

profile of v1, /device:TPU:8, one launch (start us, length us, event | category | flops | bytes accessed | tf_op | source)
XLA Modules:
  0.0 38.6 jit_solution(7191041895443643631)
XLA Ops:
  0.6 0.0 copy-start
  0.6 3.6 %moments.1 = (f32[208,128]{1,0:T(8,128)S(1)}, f32[3,32,256]{2,1,0:T(8,128)S(1)}, f32[3,16,128]{2,1,0:T(8,128)S(1)}, f32[16,512]{1,0:T(8,128)S(1)}) custom-call(f32[9,512,256]{2,1,0:T(8,128)} %bitcast.6, s32[64,128]{1,0:T(8,128)} %bitcast.8), custom_call_target="tpu_custom_call" | custom-call | flops 75497472 | bytes 4718592 | tf_op jit(solution)/shard_map/moments/pallas_call | solution.py:531
  4.3 1.6 %collective-permute-start = (f32[208,128]{1,0:T(8,128)S(1)}, f32[208,128]{1,0:T(8,128)S(1)}, u32[]{:S(2)}, u32[]{:S(2)}) collective-permute-start(f32[208,128]{1,0:T(8,128)S(1)} %get-tuple-element.18), channel_id=1, source_target_pairs={{0,16},{16,0},{32,48},{48,32},{64,80},{80,64},{96,112},{112,96},{1... | collective-permute-start | bytes 319496 | tf_op jit(solution)/shard_map/ppermute | solution.py:572
  5.9 3.2 %collective-permute-done = f32[208,128]{1,0:T(8,128)S(1)} collective-permute-done((f32[208,128]{1,0:T(8,128)S(1)}, f32[208,128]{1,0:T(8,128)S(1)}, u32[]{:S(2)}, u32[]{:S(2)}) %collective-permute-start) | collective-permute-done | bytes 106528 | tf_op jit(solution)/shard_map/ppermute | solution.py:572
  9.1 2.8 %collective-permute-start.1 = (f32[208,128]{1,0:T(8,128)S(1)}, f32[208,128]{1,0:T(8,128)S(1)}, u32[]{:S(2)}, u32[]{:S(2)}) collective-permute-start(f32[208,128]{1,0:T(8,128)S(1)} %add.9), channel_id=1, source_target_pairs={{0,48},{16,32},{32,16},{48,0},{64,112},{80,96},{96,80},{112,64},{1... | collective-permute-start | bytes 319496 | tf_op jit(solution)/shard_map/ppermute | solution.py:573
  11.9 3.7 %advect.1 = (f32[9,512,256]{2,1,0:T(8,128)S(1)}, f32[9,512,256]{2,1,0:T(8,128)S(1)}, f32[32,128]{1,0:T(8,128)S(1)}, f32[16,128]{1,0:T(8,128)S(1)}, bf16[32,640]{1,0:T(8,128)(2,1)S(1)}) custom-call(f32[9,512,256]{2,1,0:T(8,128)} %bitcast.7, bf16[32,640]{1,0:T(8,128)(2,1)} %constant.2.clone.refs_1_, f32[16,512]{1,0:T(8,128)S(1)} %get-tuple-element.19.refs_2_), custom_call_target="tpu_custom_call" | custom-call | flops 23592960 | bytes 14155776 | tf_op jit(solution)/shard_map/advect/pallas_call | solution.py:553
  15.7 0.0 collective-permute-done.1
  15.7 2.0 %collective-permute-start.2 = (f32[208,128]{1,0:T(8,128)S(1)}, f32[208,128]{1,0:T(8,128)S(1)}, u32[]{:S(2)}, u32[]{:S(2)}) collective-permute-start(f32[208,128]{1,0:T(8,128)S(1)} %add.10), channel_id=1, source_target_pairs={{0,64},{16,80},{32,96},{48,112},{64,0},{80,16},{96,32},{112,48},{1... | collective-permute-start | bytes 319496 | tf_op jit(solution)/shard_map/ppermute | solution.py:576
  17.7 1.9 %collective-permute-start.3 = (f32[3,32,256]{2,1,0:T(8,128)S(1)}, f32[3,32,256]{2,1,0:T(8,128)S(1)}, u32[]{:S(2)}, u32[]{:S(2)}) collective-permute-start(f32[3,32,256]{2,1,0:T(8,128)S(1)} %get-tuple-element.23), channel_id=1, source_target_pairs={{2,0},{4,2},{6,4},{8,6},{10,8},{12,10},{14,12},{18,16},{20,18},{22... | collective-permute-start | bytes 294920 | tf_op jit(solution)/shard_map/ppermute | solution.py:575
  19.6 0.9 %collective-permute-done.2 = f32[208,128]{1,0:T(8,128)S(1)} collective-permute-done((f32[208,128]{1,0:T(8,128)S(1)}, f32[208,128]{1,0:T(8,128)S(1)}, u32[]{:S(2)}, u32[]{:S(2)}) %collective-permute-start.2) | collective-permute-done | bytes 106528 | tf_op jit(solution)/shard_map/ppermute | solution.py:576
  20.5 1.3 %collective-permute-done.3.refs_1_ = f32[3,32,256]{2,1,0:T(8,128)S(1)} collective-permute-done((f32[3,32,256]{2,1,0:T(8,128)S(1)}, f32[3,32,256]{2,1,0:T(8,128)S(1)}, u32[]{:S(2)}, u32[]{:S(2)}) %collective-permute-start.3) | collective-permute-done | bytes 98336 | tf_op jit(solution)/shard_map/ppermute | solution.py:575
  21.8 5.1 %collective-permute-start.4 = (f32[208,128]{1,0:T(8,128)S(1)}, f32[208,128]{1,0:T(8,128)S(1)}, u32[]{:S(2)}, u32[]{:S(2)}) collective-permute-start(f32[208,128]{1,0:T(8,128)S(1)} %add.11.refs_0_), channel_id=1, source_target_pairs={{0,128},{16,144},{32,160},{48,176},{64,192},{80,208},{96,224},{112... | collective-permute-start | bytes 319496 | tf_op jit(solution)/shard_map/ppermute | solution.py:578
  26.9 4.5 %collective-permute-start.5 = (f32[3,16,128]{2,1,0:T(8,128)S(1)}, f32[3,16,128]{2,1,0:T(8,128)S(1)}, u32[]{:S(2)}, u32[]{:S(2)}) collective-permute-start(f32[3,16,128]{2,1,0:T(8,128)S(1)} %get-tuple-element.28), channel_id=1, source_target_pairs={{0,1},{1,0},{2,3},{3,2},{4,5},{5,4},{6,7},{7,6},{8,9},{9,8},{10,11... | collective-permute-start | bytes 73736 | tf_op jit(solution)/shard_map/ppermute | solution.py:579
  31.4 3.2 %collective-permute-done.5.refs_2_ = f32[3,16,128]{2,1,0:T(8,128)S(1)} collective-permute-done((f32[3,16,128]{2,1,0:T(8,128)S(1)}, f32[3,16,128]{2,1,0:T(8,128)S(1)}, u32[]{:S(2)}, u32[]{:S(2)}) %collective-permute-start.5) | collective-permute-done | bytes 24608 | tf_op jit(solution)/shard_map/ppermute | solution.py:579
  34.6 0.0 copy-done
  34.6 0.1 edges.1.refs_4_
  34.7 0.0 collective-permute-done.4.refs_1_
  34.7 3.9 %relax.1 = (f32[9,512,256]{2,1,0:T(8,128)}, f32[45,16,32]{2,1,0:T(8,128)}) custom-call(f32[208,128]{1,0:T(8,128)S(1)} %add.11.refs_0_, f32[208,128]{1,0:T(8,128)S(1)} %collective-permute-done.4.refs_1_, f32[16,512]{1,0:T(8,128)S(1)} %get-tuple-element.19.refs_2_, bf16[32,640]{1,0:T(8,128)(2,1)S(1)} %get-tuple-element.25.refs_3_, ...), custom_call_target="tpu_custom_call" | custom-call | tf_op jit(solution)/shard_map/relax/pallas_call | solution.py:592
  (3 shorter events, 0.0 us)
Async XLA Ops:
  0.6 34.0 %copy-start = (f32[256]{0:T(256)S(1)}, f32[256]{0:T(256)}, u32[]{:S(2)}) copy-start(f32[256]{0:T(256)} %param.6) | copy-start | bytes 3076
  4.3 4.8 %collective-permute-start = (f32[208,128]{1,0:T(8,128)S(1)}, f32[208,128]{1,0:T(8,128)S(1)}, u32[]{:S(2)}, u32[]{:S(2)}) collective-permute-start(f32[208,128]{1,0:T(8,128)S(1)} %get-tuple-element.18), channel_id=1, source_target_pairs={{0,16},{16,0},{32,48},{48,32},{64,80},{80,64},{96,112},{112,96},{1... | collective-permute-start | bytes 319496 | tf_op jit(solution)/shard_map/ppermute | solution.py:572
  9.1 6.6 %collective-permute-start.1 = (f32[208,128]{1,0:T(8,128)S(1)}, f32[208,128]{1,0:T(8,128)S(1)}, u32[]{:S(2)}, u32[]{:S(2)}) collective-permute-start(f32[208,128]{1,0:T(8,128)S(1)} %add.9), channel_id=1, source_target_pairs={{0,48},{16,32},{32,16},{48,0},{64,112},{80,96},{96,80},{112,64},{1... | collective-permute-start | bytes 319496 | tf_op jit(solution)/shard_map/ppermute | solution.py:573
  15.7 4.8 %collective-permute-start.2 = (f32[208,128]{1,0:T(8,128)S(1)}, f32[208,128]{1,0:T(8,128)S(1)}, u32[]{:S(2)}, u32[]{:S(2)}) collective-permute-start(f32[208,128]{1,0:T(8,128)S(1)} %add.10), channel_id=1, source_target_pairs={{0,64},{16,80},{32,96},{48,112},{64,0},{80,16},{96,32},{112,48},{1... | collective-permute-start | bytes 319496 | tf_op jit(solution)/shard_map/ppermute | solution.py:576
  17.7 4.1 %collective-permute-start.3 = (f32[3,32,256]{2,1,0:T(8,128)S(1)}, f32[3,32,256]{2,1,0:T(8,128)S(1)}, u32[]{:S(2)}, u32[]{:S(2)}) collective-permute-start(f32[3,32,256]{2,1,0:T(8,128)S(1)} %get-tuple-element.23), channel_id=1, source_target_pairs={{2,0},{4,2},{6,4},{8,6},{10,8},{12,10},{14,12},{18,16},{20,18},{22... | collective-permute-start | bytes 294920 | tf_op jit(solution)/shard_map/ppermute | solution.py:575
  21.8 12.9 %collective-permute-start.4 = (f32[208,128]{1,0:T(8,128)S(1)}, f32[208,128]{1,0:T(8,128)S(1)}, u32[]{:S(2)}, u32[]{:S(2)}) collective-permute-start(f32[208,128]{1,0:T(8,128)S(1)} %add.11.refs_0_), channel_id=1, source_target_pairs={{0,128},{16,144},{32,160},{48,176},{64,192},{80,208},{96,224},{112... | collective-permute-start | bytes 319496 | tf_op jit(solution)/shard_map/ppermute | solution.py:578
  26.9 7.7 %collective-permute-start.5 = (f32[3,16,128]{2,1,0:T(8,128)S(1)}, f32[3,16,128]{2,1,0:T(8,128)S(1)}, u32[]{:S(2)}, u32[]{:S(2)}) collective-permute-start(f32[3,16,128]{2,1,0:T(8,128)S(1)} %get-tuple-element.28), channel_id=1, source_target_pairs={{0,1},{1,0},{2,3},{3,2},{4,5},{5,4},{6,7},{7,6},{8,9},{9,8},{10,11... | collective-permute-start | bytes 73736 | tf_op jit(solution)/shard_map/ppermute | solution.py:579

commit v2 on v1

--- a/solution.py
+++ b/solution.py
@@ -22,6 +22,7 @@
 TAIL = 160
 COEF_ROWS = 32
 MASK_ROWS = 16
+GROUPS = [(0, 3), (3, 6), (6, 9)]
 CHUNKS = 4
 F32 = jnp.float32
 BF16 = jnp.bfloat16
@@ -148,11 +149,13 @@
 
 def moments_kernel(wx, wy, dist, kinds, sums, face_x, face_y, masks, dv, kind, sems):
     n = wx * wy
-    copies = [pltpu.make_async_copy(dist.at[k], dv.at[k], sems.at[k]) for k in range(9)]
+    copies = {
+        first: pltpu.make_async_copy(dist.at[first:last], dv.at[first:last], sems.at[first])
+        for first, last in GROUPS
+    }
     kind_copy = pltpu.make_async_copy(kinds, kind, sems.at[9])
-    copies[0].start()
     kind_copy.start()
-    for copy in copies[1:]:
+    for copy in copies.values():
         copy.start()
     level, vx = own_speed()
     sums[...] = jnp.zeros_like(sums)
@@ -170,7 +173,8 @@
     walls_x, walls_y = [None] * 3, [None] * 3
     for k in range(9):
         i, j = divmod(k, 3)
-        copies[k].wait()
+        if k in copies:
+            copies[k].wait()
         plane = dv[k]
         high = plane.astype(BF16)
         low = (plane - high.astype(F32)).astype(BF16)
@@ -331,11 +335,10 @@
     keep.wait()
 
 
-def edges_kernel(wx, wy, inside, halo_x, halo_y, inflow, edge_x, edge_y, out):
+def edges_kernel(wx, wy, inside, halo_x, inflow, edge_x, out):
     del inside
     level, _ = own_speed()
     forward = level >= NV // 2
-    upper = lax.axis_index("gy") != 0
     first_x = lax.axis_index("gx") == 0
 
     def along_x(p, i, outside):
@@ -345,27 +348,43 @@
                 lanes = slice(half * HALF, (half + 1) * HALF)
                 out[3 * i + j, rows, lanes] += edge_x[...] * outside(j, lanes)
 
-    def along_y(q, j, lanes):
+    @pl.when(forward)
+    def _():
+        along_x(0, 0, lambda j, at: jnp.where(first_x, inflow[:, at], halo_x[j, :, at]))
+
+    @pl.when(jnp.logical_not(forward))
+    def _():
+        along_x(wx - 1, 2, lambda j, at: halo_x[j, :, at])
+
+
+def rows_kernel(wx, wy, inside, rows, halo_y, edge_y, out, fresh, sem):
+    del inside
+    upper = lax.axis_index("gy") != 0
+
+    def write(row, first, face, half):
+        fresh[...] = rows[...]
         for i in range(3):
             for p in range(wx):
-                at = slice(p * wy + q, p * wy + q + 1)
-                out[3 * i + j, at, lanes] += edge_y[p : p + 1, :] * halo_y[i, p : p + 1, :]
-
-    @pl.when(forward)
-    def _():
-        along_x(0, 0, lambda j, at: jnp.where(first_x, inflow[:, at], halo_x[j, :, at]))
-
-    @pl.when(jnp.logical_not(forward))
-    def _():
-        along_x(wx - 1, 2, lambda j, at: halo_x[j, :, at])
+                fresh[i, p, row : row + 1, :] += edge_y[p : p + 1, :] * halo_y[i, p : p + 1, :]
+        lanes = slice(half * HALF, (half + 1) * HALF)
+        copies = [
+            pltpu.make_async_copy(
+                fresh.at[i], out.at[3 * i + face, :, first : first + 8, lanes], sem.at[i]
+            )
+            for i in range(3)
+        ]
+        for copy in copies:
+            copy.start()
+        for copy in copies:
+            copy.wait()
 
     @pl.when(upper)
     def _():
-        along_y(0, 0, slice(HALF, LANES))
+        write(0, 0, 0, 1)
 
     @pl.when(jnp.logical_not(upper))
     def _():
-        along_y(wy - 1, 2, slice(0, HALF))
+        write(7, wy - 8, 2, 0)
 
 
 def split(value, count):
@@ -388,6 +407,7 @@
     dv,
     out,
     fields_out,
+    border,
     coef,
     fields,
     result,
@@ -465,7 +485,8 @@
         store_wall(3 * i + 2, 23, solid_a * value)
 
     weights = table[...]
-    chunk = min(256, n)
+    chunk = 128
+    block = 2 * chunk
     copies = []
     for k in range(9):
         for start in range(0, n, chunk):
@@ -484,9 +505,29 @@
                 result[k, rows, lanes] = (
                     advected[k, rows, lanes] - rate * dv[k, rows, lanes] + (target + wall)
                 )
-        copy = pltpu.make_async_copy(result.at[k], out.at[k], sems.at[k])
-        copy.start()
-        copies.append(copy)
+            if (start + chunk) % block == 0:
+                done = slice(start + chunk - block, start + chunk)
+                copy = pltpu.make_async_copy(
+                    result.at[k, done], out.at[k, done], sems.at[len(copies)]
+                )
+                copy.start()
+                copies.append(copy)
+    upper = lax.axis_index("gy") != 0
+
+    def keep(first, face, half):
+        for i in range(3):
+            for p in range(wx):
+                at = slice(p * wy + first, p * wy + first + 8)
+                border[i, p] = result[3 * i + face, at, half * HALF : (half + 1) * HALF]
+
+    @pl.when(upper)
+    def _():
+        keep(0, 0, 1)
+
+    @pl.when(jnp.logical_not(upper))
+    def _():
+        keep(wy - 8, 2, 0)
+
     for p in range(wx):
         fields_out[:, p, :] = fields[0:45, p * wy : (p + 1) * wy]
     for copy in copies:
@@ -575,44 +616,45 @@
     halo_x = lax.ppermute(face_x, ("vel", "gx"), upwind_pairs())
     total = total + lax.ppermute(total, "vel", steps[2])
     total, halo_x = lax.optimization_barrier((total, halo_x))
-    other = lax.ppermute(total, "vel", steps[3])
-    halo_y = lax.ppermute(face_y, "gy", [(0, 1), (1, 0)])
     advected = pl.pallas_call(
         lambda *refs: edges_kernel(wx, wy, *refs),
         out_shape=vmem((9, n, LANES)),
-        in_specs=[whole] * 6,
+        in_specs=[whole] * 4,
         out_specs=whole,
         input_output_aliases={0: 0},
         compiler_params=pltpu.CompilerParams(vmem_limit_bytes=4 << 20),
-        cost_estimate=pl.CostEstimate(
-            flops=100 * 9 * n * LANES, bytes_accessed=40 * 9 * n * LANES, transcendentals=0
-        ),
         name="edges",
-    )(in_vmem(advected), halo_x, halo_y, inflow[None, :], edge_x, edge_y)
-    fresh, fields = pl.pallas_call(
+    )(in_vmem(advected), halo_x, inflow[None, :], edge_x)
+    other = lax.ppermute(total, "vel", steps[3])
+    halo_y = lax.ppermute(face_y, "gy", [(0, 1), (1, 0)])
+    fresh, fields, border = pl.pallas_call(
         lambda *refs: relax_kernel(wx, wy, *refs),
         out_shape=(
             jax.ShapeDtypeStruct((9, n, LANES), F32),
             jax.ShapeDtypeStruct((45, wx, wy), F32),
+            vmem((3, wx, 8, HALF)),
         ),
         in_specs=[whole] * 6,
-        out_specs=(anywhere, whole),
+        out_specs=(anywhere, whole, whole),
         scratch_shapes=[
             pltpu.VMEM((9, COEF_ROWS, n), F32),
             pltpu.VMEM((48, n), F32),
             pltpu.VMEM((9, n, LANES), F32),
-            pltpu.SemaphoreType.DMA((9,)),
+            pltpu.SemaphoreType.DMA((9 * n // 256,)),
         ],
         compiler_params=pltpu.CompilerParams(vmem_limit_bytes=16 << 20),
         name="relax",
-    )(
-        total,
-        other,
-        masks,
-        table,
-        in_vmem(advected),
-        in_vmem(held),
-    )
+    )(total, other, masks, table, in_vmem(advected), in_vmem(held))
+    fresh = pl.pallas_call(
+        lambda *refs: rows_kernel(wx, wy, *refs),
+        out_shape=jax.ShapeDtypeStruct((9, wx, wy, LANES), F32),
+        in_specs=[anywhere, whole, whole, whole],
+        out_specs=anywhere,
+        scratch_shapes=[pltpu.VMEM((3, wx, 8, HALF), F32), pltpu.SemaphoreType.DMA((3,))],
+        input_output_aliases={0: 0},
+        compiler_params=pltpu.CompilerParams(vmem_limit_bytes=4 << 20),
+        name="rows",
+    )(fresh.reshape(9, wx, wy, LANES), border, halo_y, edge_y)
     return (fresh.reshape(dist.shape), fields.reshape(5, 3, 3, wx, wy))
 
 

time: 38.7 us -> 35.7 us (0.922)
  waiting for transfers between devices: 8.64 us -> 5.4 us
    ppermute x1, waiting for transfers between devices: 3.24 us -> 0.01 us  [shards(): halo_y = lax.ppermute(face_y, 'gy', [(0, 1), (1, 0)])]
    pallas_call x0 -> x1, Pallas kernels: none -> 0.76 us  [shards(): pl.pallas_call(lambda *refs: rows_kernel(wx, wy, *refs), out_shape=jax.Sh...]
    pallas_call x1, Pallas kernels: 3.64 us -> 3.16 us  [shards(): pl.pallas_call(lambda *refs: moments_kernel(wx, wy, *refs), out_shape=(vm...]
  transfers between devices with their start and end apart: 6 -> 6, of which waited for: 4 -> 3; matrix products, arithmetic and copies ran while one was open for 0% -> 0% of each run, Pallas kernels for 10% -> 21%
where the time goes in v2:
time: 35.7 us; the launch traced here: 35.4 us
  starting transfers between devices  17.9 us (50%)
  Pallas kernels  11.3 us (32%)
  waiting for transfers between devices  5.4 us (15%)
  between operations  0.72 us (2%)
    ppermute x1, starting transfers between devices, shards(): other = lax.ppermute(total, 'vel', steps[3])  5.09 us
    ppermute x1, starting transfers between devices, shards(): halo_y = lax.ppermute(face_y, 'gy', [(0, 1), (1, 0)])  4.49 us
    pallas_call x1, Pallas kernels, shards(): pl.pallas_call(lambda *refs: advect_kernel(wx, wy, *refs), out_shape=(vme...  3.7 us
    pallas_call x1, Pallas kernels, shards(): pl.pallas_call(lambda *refs: relax_kernel(wx, wy, *refs), out_shape=(jax....  3.68 us
    ppermute x1, waiting for transfers between devices, shards(): total = sums + lax.ppermute(sums, 'vel', steps[0])  3.22 us
    pallas_call x1, Pallas kernels, shards(): pl.pallas_call(lambda *refs: moments_kernel(wx, wy, *refs), out_shape=(vm...  3.16 us
    ppermute x1, starting transfers between devices, shards(): total = total + lax.ppermute(total, 'vel', steps[1])  2.85 us
    ppermute x1, starting transfers between devices, shards(): total = total + lax.ppermute(total, 'vel', steps[2])  2 us
  transfers between devices with their start and end apart: 6, of which 3 were waited for; matrix products, arithmetic and copies ran while one was open for 0% of the time, Pallas kernels for 21%

profile of v2, /device:TPU:8, one launch (start us, length us, event | category | flops | bytes accessed | tf_op | source)
XLA Modules:
  0.0 35.4 jit_solution(7530855156395470079)
XLA Ops:
  0.6 0.0 copy-start
  0.6 3.2 %moments.1 = (f32[208,128]{1,0:T(8,128)S(1)}, f32[3,32,256]{2,1,0:T(8,128)S(1)}, f32[3,16,128]{2,1,0:T(8,128)S(1)}, f32[16,512]{1,0:T(8,128)S(1)}) custom-call(f32[9,512,256]{2,1,0:T(8,128)} %bitcast.7, s32[64,128]{1,0:T(8,128)} %bitcast.11), custom_call_target="tpu_custom_call" | custom-call | flops 75497472 | bytes 4718592 | tf_op jit(solution)/shard_map/moments/pallas_call | solution.py:572
  3.8 1.6 %collective-permute-start = (f32[208,128]{1,0:T(8,128)S(1)}, f32[208,128]{1,0:T(8,128)S(1)}, u32[]{:S(2)}, u32[]{:S(2)}) collective-permute-start(f32[208,128]{1,0:T(8,128)S(1)} %get-tuple-element.19), channel_id=1, source_target_pairs={{0,16},{16,0},{32,48},{48,32},{64,80},{80,64},{96,112},{112,96},{1... | collective-permute-start | bytes 319496 | tf_op jit(solution)/shard_map/ppermute | solution.py:613
  5.4 3.2 %collective-permute-done = f32[208,128]{1,0:T(8,128)S(1)} collective-permute-done((f32[208,128]{1,0:T(8,128)S(1)}, f32[208,128]{1,0:T(8,128)S(1)}, u32[]{:S(2)}, u32[]{:S(2)}) %collective-permute-start) | collective-permute-done | bytes 106528 | tf_op jit(solution)/shard_map/ppermute | solution.py:613
  8.6 2.8 %collective-permute-start.1 = (f32[208,128]{1,0:T(8,128)S(1)}, f32[208,128]{1,0:T(8,128)S(1)}, u32[]{:S(2)}, u32[]{:S(2)}) collective-permute-start(f32[208,128]{1,0:T(8,128)S(1)} %add.9), channel_id=1, source_target_pairs={{0,48},{16,32},{32,16},{48,0},{64,112},{80,96},{96,80},{112,64},{1... | collective-permute-start | bytes 319496 | tf_op jit(solution)/shard_map/ppermute | solution.py:614
  11.5 3.7 %advect.1 = (f32[9,512,256]{2,1,0:T(8,128)S(1)}, f32[9,512,256]{2,1,0:T(8,128)S(1)}, f32[32,128]{1,0:T(8,128)S(1)}, f32[16,128]{1,0:T(8,128)S(1)}, bf16[32,640]{1,0:T(8,128)(2,1)S(1)}) custom-call(f32[9,512,256]{2,1,0:T(8,128)} %bitcast.8, bf16[32,640]{1,0:T(8,128)(2,1)} %constant.2.clone.refs_1_, f32[16,512]{1,0:T(8,128)S(1)} %get-tuple-element.20.refs_2_), custom_call_target="tpu_custom_call" | custom-call | flops 23592960 | bytes 14155776 | tf_op jit(solution)/shard_map/advect/pallas_call | solution.py:594
  15.2 0.0 collective-permute-done.1
  15.2 2.0 %collective-permute-start.2 = (f32[208,128]{1,0:T(8,128)S(1)}, f32[208,128]{1,0:T(8,128)S(1)}, u32[]{:S(2)}, u32[]{:S(2)}) collective-permute-start(f32[208,128]{1,0:T(8,128)S(1)} %add.10), channel_id=1, source_target_pairs={{0,64},{16,80},{32,96},{48,112},{64,0},{80,16},{96,32},{112,48},{1... | collective-permute-start | bytes 319496 | tf_op jit(solution)/shard_map/ppermute | solution.py:617
  17.2 1.9 %collective-permute-start.3 = (f32[3,32,256]{2,1,0:T(8,128)S(1)}, f32[3,32,256]{2,1,0:T(8,128)S(1)}, u32[]{:S(2)}, u32[]{:S(2)}) collective-permute-start(f32[3,32,256]{2,1,0:T(8,128)S(1)} %get-tuple-element.24), channel_id=1, source_target_pairs={{2,0},{4,2},{6,4},{8,6},{10,8},{12,10},{14,12},{18,16},{20,18},{22... | collective-permute-start | bytes 294920 | tf_op jit(solution)/shard_map/ppermute | solution.py:616
  19.1 0.9 %collective-permute-done.2 = f32[208,128]{1,0:T(8,128)S(1)} collective-permute-done((f32[208,128]{1,0:T(8,128)S(1)}, f32[208,128]{1,0:T(8,128)S(1)}, u32[]{:S(2)}, u32[]{:S(2)}) %collective-permute-start.2) | collective-permute-done | bytes 106528 | tf_op jit(solution)/shard_map/ppermute | solution.py:617
  20.0 1.3 %collective-permute-done.3.refs_1_ = f32[3,32,256]{2,1,0:T(8,128)S(1)} collective-permute-done((f32[3,32,256]{2,1,0:T(8,128)S(1)}, f32[3,32,256]{2,1,0:T(8,128)S(1)}, u32[]{:S(2)}, u32[]{:S(2)}) %collective-permute-start.3) | collective-permute-done | bytes 98336 | tf_op jit(solution)/shard_map/ppermute | solution.py:616
  21.3 5.1 %collective-permute-start.4 = (f32[208,128]{1,0:T(8,128)S(1)}, f32[208,128]{1,0:T(8,128)S(1)}, u32[]{:S(2)}, u32[]{:S(2)}) collective-permute-start(f32[208,128]{1,0:T(8,128)S(1)} %add.11.refs_0_), channel_id=1, source_target_pairs={{0,128},{16,144},{32,160},{48,176},{64,192},{80,208},{96,224},{112... | collective-permute-start | bytes 319496 | tf_op jit(solution)/shard_map/ppermute | solution.py:628
  26.4 4.5 %collective-permute-start.5 = (f32[3,16,128]{2,1,0:T(8,128)S(1)}, f32[3,16,128]{2,1,0:T(8,128)S(1)}, u32[]{:S(2)}, u32[]{:S(2)}) collective-permute-start(f32[3,16,128]{2,1,0:T(8,128)S(1)} %get-tuple-element.33), channel_id=1, source_target_pairs={{0,1},{1,0},{2,3},{3,2},{4,5},{5,4},{6,7},{7,6},{8,9},{9,8},{10,11... | collective-permute-start | bytes 73736 | tf_op jit(solution)/shard_map/ppermute | solution.py:629
  30.9 0.0 copy-done
  30.9 0.0 collective-permute-done.4.refs_1_
  30.9 3.7 %relax.1 = (f32[9,512,256]{2,1,0:T(8,128)}, f32[45,16,32]{2,1,0:T(8,128)}, f32[3,16,8,128]{3,2,1,0:T(8,128)S(1)}) custom-call(f32[208,128]{1,0:T(8,128)S(1)} %add.11.refs_0_, f32[208,128]{1,0:T(8,128)S(1)} %collective-permute-done.4.refs_1_, f32[16,512]{1,0:T(8,128)S(1)} %get-tuple-element.20.refs_2_, bf16[32,640]{1,0:T(8,128)(2,1)S(1)} %get-tuple-element.26.refs_3_, ...), custom_call_target="tpu_custom_call" | custom-call | tf_op jit(solution)/shard_map/relax/pallas_call | solution.py:630
  34.6 0.0 collective-permute-done.5.refs_2_
  34.6 0.8 %rows.1 = f32[9,16,32,256]{3,2,1,0:T(8,128)} custom-call(f32[9,16,32,256]{3,2,1,0:T(8,128)} %bitcast.9, f32[3,16,8,128]{3,2,1,0:T(8,128)S(1)} %get-tuple-element.32.refs_1_, f32[3,16,128]{2,1,0:T(8,128)S(1)} %collective-permute-done.5.refs_2_, f32[16,128]{1,0:T(8,128)S(1)} %get-tuple-element.34.refs_3_), custom_call_target="tpu_custom_call", output_to_operand_aliasing={{}: (0, {})} | custom-call | tf_op jit(solution)/shard_map/rows/pallas_call | solution.py:648
  (4 shorter events, 0.1 us)
Async XLA Ops:
  0.6 30.3 %copy-start = (f32[256]{0:T(256)S(1)}, f32[256]{0:T(256)}, u32[]{:S(2)}) copy-start(f32[256]{0:T(256)} %param.6) | copy-start | bytes 3076
  3.8 4.8 %collective-permute-start = (f32[208,128]{1,0:T(8,128)S(1)}, f32[208,128]{1,0:T(8,128)S(1)}, u32[]{:S(2)}, u32[]{:S(2)}) collective-permute-start(f32[208,128]{1,0:T(8,128)S(1)} %get-tuple-element.19), channel_id=1, source_target_pairs={{0,16},{16,0},{32,48},{48,32},{64,80},{80,64},{96,112},{112,96},{1... | collective-permute-start | bytes 319496 | tf_op jit(solution)/shard_map/ppermute | solution.py:613
  8.6 6.6 %collective-permute-start.1 = (f32[208,128]{1,0:T(8,128)S(1)}, f32[208,128]{1,0:T(8,128)S(1)}, u32[]{:S(2)}, u32[]{:S(2)}) collective-permute-start(f32[208,128]{1,0:T(8,128)S(1)} %add.9), channel_id=1, source_target_pairs={{0,48},{16,32},{32,16},{48,0},{64,112},{80,96},{96,80},{112,64},{1... | collective-permute-start | bytes 319496 | tf_op jit(solution)/shard_map/ppermute | solution.py:614
  15.2 4.8 %collective-permute-start.2 = (f32[208,128]{1,0:T(8,128)S(1)}, f32[208,128]{1,0:T(8,128)S(1)}, u32[]{:S(2)}, u32[]{:S(2)}) collective-permute-start(f32[208,128]{1,0:T(8,128)S(1)} %add.10), channel_id=1, source_target_pairs={{0,64},{16,80},{32,96},{48,112},{64,0},{80,16},{96,32},{112,48},{1... | collective-permute-start | bytes 319496 | tf_op jit(solution)/shard_map/ppermute | solution.py:617
  17.2 4.1 %collective-permute-start.3 = (f32[3,32,256]{2,1,0:T(8,128)S(1)}, f32[3,32,256]{2,1,0:T(8,128)S(1)}, u32[]{:S(2)}, u32[]{:S(2)}) collective-permute-start(f32[3,32,256]{2,1,0:T(8,128)S(1)} %get-tuple-element.24), channel_id=1, source_target_pairs={{2,0},{4,2},{6,4},{8,6},{10,8},{12,10},{14,12},{18,16},{20,18},{22... | collective-permute-start | bytes 294920 | tf_op jit(solution)/shard_map/ppermute | solution.py:616
  21.3 9.6 %collective-permute-start.4 = (f32[208,128]{1,0:T(8,128)S(1)}, f32[208,128]{1,0:T(8,128)S(1)}, u32[]{:S(2)}, u32[]{:S(2)}) collective-permute-start(f32[208,128]{1,0:T(8,128)S(1)} %add.11.refs_0_), channel_id=1, source_target_pairs={{0,128},{16,144},{32,160},{48,176},{64,192},{80,208},{96,224},{112... | collective-permute-start | bytes 319496 | tf_op jit(solution)/shard_map/ppermute | solution.py:628
  26.4 8.2 %collective-permute-start.5 = (f32[3,16,128]{2,1,0:T(8,128)S(1)}, f32[3,16,128]{2,1,0:T(8,128)S(1)}, u32[]{:S(2)}, u32[]{:S(2)}) collective-permute-start(f32[3,16,128]{2,1,0:T(8,128)S(1)} %get-tuple-element.33), channel_id=1, source_target_pairs={{0,1},{1,0},{2,3},{3,2},{4,5},{5,4},{6,7},{7,6},{8,9},{9,8},{10,11... | collective-permute-start | bytes 73736 | tf_op jit(solution)/shard_map/ppermute | solution.py:629

commit v3 on v2

--- a/solution.py
+++ b/solution.py
@@ -23,6 +23,8 @@
 COEF_ROWS = 32
 MASK_ROWS = 16
 GROUPS = [(0, 3), (3, 6), (6, 9)]
+ORDERS = ((1, 3, 4, 8), (4, 8, 1, 3))
+SLOT = slice(TAIL + 20, TAIL + 32)
 CHUNKS = 4
 F32 = jnp.float32
 BF16 = jnp.bfloat16
@@ -426,8 +428,8 @@
     def both(rows):
         return sums_a[rows, :] + sums_b[rows, :]
 
-    def received(rows):
-        return sums_b[rows, :]
+    def slot(rows):
+        return jnp.where(lax.axis_index("gx") % 2 == 1, both(rows), sums_b[rows, :])
 
     fluid = masks[0:1, :]
     coef[...] = jnp.zeros_like(coef)
@@ -476,7 +478,7 @@
     solid_b = masks[8:9, :] * gauss_x
     solid_a = masks[9:10, :] * gauss_x
     for j in range(3):
-        value = solid_x * wide(received, TAIL + (5 + j) * 4, 1, 1)
+        value = solid_x * wide(slot, TAIL + (5 + j) * 4, 1, 1)
         store_wall(j, 17, value * forward)
         store_wall(6 + j, 17, value * (1.0 - forward))
     for i in range(3):
@@ -535,12 +537,14 @@
 
 
 def exchanges():
-    count = lax.axis_size("vel")
-    return (
-        [(v, v ^ 1) for v in range(count)],
-        [(v, v ^ 3) for v in range(count)],
-        [(v, v ^ 4) for v in range(count)],
-        [(v, v ^ 8) for v in range(count)],
+    count, columns = lax.axis_size("vel"), lax.axis_size("gx")
+    return tuple(
+        [
+            (v * columns + g, (v ^ steps[g % 2]) * columns + g)
+            for v in range(count)
+            for g in range(columns)
+        ]
+        for steps in zip(*ORDERS)
     )
 
 
@@ -610,12 +614,18 @@
         name="advect",
     )(planes, pltpu.with_memory_space_constraint(table, pltpu.HBM), masks)
     steps = exchanges()
-    total = sums + lax.ppermute(sums, "vel", steps[0])
-    total = total + lax.ppermute(total, "vel", steps[1])
+    def partner(value, pairs):
+        return lax.ppermute(value, ("vel", "gx"), pairs)
+
+    odd = lax.axis_index("gx") % 2 == 1
+    row = jnp.arange(SUM_ROWS, dtype=jnp.int32)[:, None]
+    swapped = jnp.logical_and(odd, jnp.logical_and(row >= SLOT.start, row < SLOT.stop))
+    total = sums + partner(sums, steps[0])
+    total = jnp.where(swapped, 0.0, total) + partner(total, steps[1])
+    halo_x = lax.ppermute(face_x, ("vel", "gx"), upwind_pairs())
+    total, halo_x = lax.optimization_barrier((total, halo_x))
+    total = total + partner(total, steps[2])
     total, edge_x, edge_y = lax.optimization_barrier((total, edge_x, edge_y))
-    halo_x = lax.ppermute(face_x, ("vel", "gx"), upwind_pairs())
-    total = total + lax.ppermute(total, "vel", steps[2])
-    total, halo_x = lax.optimization_barrier((total, halo_x))
     advected = pl.pallas_call(
         lambda *refs: edges_kernel(wx, wy, *refs),
         out_shape=vmem((9, n, LANES)),
@@ -625,7 +635,7 @@
         compiler_params=pltpu.CompilerParams(vmem_limit_bytes=4 << 20),
         name="edges",
     )(in_vmem(advected), halo_x, inflow[None, :], edge_x)
-    other = lax.ppermute(total, "vel", steps[3])
+    other = partner(total, steps[3])
     halo_y = lax.ppermute(face_y, "gy", [(0, 1), (1, 0)])
     fresh, fields, border = pl.pallas_call(
         lambda *refs: relax_kernel(wx, wy, *refs),

time: 35.7 us -> 32.9 us (0.922)
  starting transfers between devices: 17.9 us -> 16.2 us
  waiting for transfers between devices: 5.4 us -> 4.42 us
    ppermute x4, starting transfers between devices: 11.5 us -> 9.79 us  [partner(): return lax.ppermute(value, ('vel', 'gx'), pairs)]
    ppermute x1, waiting for transfers between devices: 1.3 us -> 0.01 us  [shards(): halo_x = lax.ppermute(face_x, ('vel', 'gx'), upwind_pairs())]
  transfers between devices with their start and end apart: 6 -> 6, of which waited for: 3 -> 2; matrix products, arithmetic and copies ran while one was open for 0% -> 0% of each run, Pallas kernels for 21% -> 23%
where the time goes in v3:
time: 32.9 us; the launch traced here: 32.8 us
  starting transfers between devices  16.2 us (49%)
  Pallas kernels  11.3 us (34%)
  waiting for transfers between devices  4.42 us (13%)
  between operations  0.74 us (2%)
    ppermute x4, starting transfers between devices, partner(): return lax.ppermute(value, ('vel', 'gx'), pairs)  9.79 us
    ppermute x1, starting transfers between devices, shards(): halo_y = lax.ppermute(face_y, 'gy', [(0, 1), (1, 0)])  4.49 us
    ppermute x4, waiting for transfers between devices, partner(): return lax.ppermute(value, ('vel', 'gx'), pairs)  4.42 us
    pallas_call x1, Pallas kernels, shards(): pl.pallas_call(lambda *refs: advect_kernel(wx, wy, *refs), out_shape=(vme...  3.7 us
    pallas_call x1, Pallas kernels, shards(): pl.pallas_call(lambda *refs: relax_kernel(wx, wy, *refs), out_shape=(jax....  3.69 us
    pallas_call x1, Pallas kernels, shards(): pl.pallas_call(lambda *refs: moments_kernel(wx, wy, *refs), out_shape=(vm...  3.16 us
    ppermute x1, starting transfers between devices, shards(): halo_x = lax.ppermute(face_x, ('vel', 'gx'), upwind_pairs())  1.93 us
    pallas_call x1, Pallas kernels, shards(): pl.pallas_call(lambda *refs: rows_kernel(wx, wy, *refs), out_shape=jax.Sh...  0.76 us
  transfers between devices with their start and end apart: 6, of which 2 were waited for; matrix products, arithmetic and copies ran while one was open for 0% of the time, Pallas kernels for 23%

profile of v3, /device:TPU:8, one launch (start us, length us, event | category | flops | bytes accessed | tf_op | source)
XLA Modules:
  0.0 32.8 jit_solution(17015818345211911821)
XLA Ops:
  0.6 0.0 copy-start
  0.6 3.2 %moments.1 = (f32[208,128]{1,0:T(8,128)S(1)}, f32[3,32,256]{2,1,0:T(8,128)S(1)}, f32[3,16,128]{2,1,0:T(8,128)S(1)}, f32[16,512]{1,0:T(8,128)S(1)}) custom-call(f32[9,512,256]{2,1,0:T(8,128)} %bitcast.7, s32[64,128]{1,0:T(8,128)} %bitcast.11), custom_call_target="tpu_custom_call" | custom-call | flops 75497472 | bytes 4718592 | tf_op jit(solution)/shard_map/moments/pallas_call | solution.py:576
  3.8 1.6 %collective-permute-start = (f32[208,128]{1,0:T(8,128)S(1)}, f32[208,128]{1,0:T(8,128)S(1)}, u32[]{:S(2)}, u32[]{:S(2)}) collective-permute-start(f32[208,128]{1,0:T(8,128)S(1)} %get-tuple-element.19), channel_id=1, source_target_pairs={{0,16},{2,66},{4,20},{6,70},{8,24},{10,74},{12,28},{14,78},{16,0},... | collective-permute-start | bytes 319496 | tf_op jit(solution)/shard_map/ppermute | solution.py:618
  5.4 1.9 %collective-permute-start.2 = (f32[3,32,256]{2,1,0:T(8,128)S(1)}, f32[3,32,256]{2,1,0:T(8,128)S(1)}, u32[]{:S(2)}, u32[]{:S(2)}) collective-permute-start(f32[3,32,256]{2,1,0:T(8,128)S(1)} %get-tuple-element.20), channel_id=1, source_target_pairs={{2,0},{4,2},{6,4},{8,6},{10,8},{12,10},{14,12},{18,16},{20,18},{22... | collective-permute-start | bytes 294920 | tf_op jit(solution)/shard_map/ppermute | solution.py:625
  7.3 1.3 %collective-permute-done = f32[208,128]{1,0:T(8,128)S(1)} collective-permute-done((f32[208,128]{1,0:T(8,128)S(1)}, f32[208,128]{1,0:T(8,128)S(1)}, u32[]{:S(2)}, u32[]{:S(2)}) %collective-permute-start) | collective-permute-done | bytes 106528 | tf_op jit(solution)/shard_map/ppermute | solution.py:618
  8.6 2.8 %collective-permute-start.1 = (f32[208,128]{1,0:T(8,128)S(1)}, f32[208,128]{1,0:T(8,128)S(1)}, u32[]{:S(2)}, u32[]{:S(2)}) collective-permute-start(f32[208,128]{1,0:T(8,128)S(1)} %add.14), channel_id=1, source_target_pairs={{0,48},{2,130},{4,52},{6,134},{8,56},{10,138},{12,60},{14,142},{16... | collective-permute-start | bytes 319496 | tf_op jit(solution)/shard_map/ppermute | solution.py:618
  11.5 3.1 %collective-permute-done.1 = f32[208,128]{1,0:T(8,128)S(1)} collective-permute-done((f32[208,128]{1,0:T(8,128)S(1)}, f32[208,128]{1,0:T(8,128)S(1)}, u32[]{:S(2)}, u32[]{:S(2)}) %collective-permute-start.1) | collective-permute-done | bytes 106528 | tf_op jit(solution)/shard_map/ppermute | solution.py:618
  14.6 0.1 select_add_fusion
  14.7 0.0 collective-permute-done.2.refs_1_
  14.7 2.0 %collective-permute-start.3 = (f32[208,128]{1,0:T(8,128)S(1)}, f32[208,128]{1,0:T(8,128)S(1)}, u32[]{:S(2)}, u32[]{:S(2)}) collective-permute-start(f32[208,128]{1,0:T(8,128)S(1)} %select_add_fusion), channel_id=1, source_target_pairs={{0,64},{2,18},{4,68},{6,22},{8,72},{10,26},{12,76},{14,30},{16,80}... | collective-permute-start | bytes 319496 | tf_op jit(solution)/shard_map/ppermute | solution.py:618
  16.7 3.7 %advect.1 = (f32[9,512,256]{2,1,0:T(8,128)S(1)}, f32[9,512,256]{2,1,0:T(8,128)S(1)}, f32[32,128]{1,0:T(8,128)S(1)}, f32[16,128]{1,0:T(8,128)S(1)}, bf16[32,640]{1,0:T(8,128)(2,1)S(1)}) custom-call(f32[9,512,256]{2,1,0:T(8,128)} %bitcast.8, bf16[32,640]{1,0:T(8,128)(2,1)} %constant.28.clone.refs_1_, f32[16,512]{1,0:T(8,128)S(1)} %get-tuple-element.22.refs_2_), custom_call_target="tpu_custom_call" | custom-call | flops 23592960 | bytes 14155776 | tf_op jit(solution)/shard_map/advect/pallas_call | solution.py:598
  20.4 0.0 collective-permute-done.3
  20.5 3.4 %collective-permute-start.4 = (f32[208,128]{1,0:T(8,128)S(1)}, f32[208,128]{1,0:T(8,128)S(1)}, u32[]{:S(2)}, u32[]{:S(2)}) collective-permute-start(f32[208,128]{1,0:T(8,128)S(1)} %add.16.refs_0_), channel_id=1, source_target_pairs={{0,128},{2,50},{4,132},{6,54},{8,136},{10,58},{12,140},{14,62},{16... | collective-permute-start | bytes 319496 | tf_op jit(solution)/shard_map/ppermute | solution.py:618
  23.8 4.5 %collective-permute-start.5 = (f32[3,16,128]{2,1,0:T(8,128)S(1)}, f32[3,16,128]{2,1,0:T(8,128)S(1)}, u32[]{:S(2)}, u32[]{:S(2)}) collective-permute-start(f32[3,16,128]{2,1,0:T(8,128)S(1)} %get-tuple-element.33), channel_id=1, source_target_pairs={{0,1},{1,0},{2,3},{3,2},{4,5},{5,4},{6,7},{7,6},{8,9},{9,8},{10,11... | collective-permute-start | bytes 73736 | tf_op jit(solution)/shard_map/ppermute | solution.py:639
  28.3 0.0 copy-done
  28.4 0.0 collective-permute-done.4.refs_1_
  28.4 3.7 %relax.1 = (f32[9,512,256]{2,1,0:T(8,128)}, f32[45,16,32]{2,1,0:T(8,128)}, f32[3,16,8,128]{3,2,1,0:T(8,128)S(1)}) custom-call(f32[208,128]{1,0:T(8,128)S(1)} %add.16.refs_0_, f32[208,128]{1,0:T(8,128)S(1)} %collective-permute-done.4.refs_1_, f32[16,512]{1,0:T(8,128)S(1)} %get-tuple-element.22.refs_2_, bf16[32,640]{1,0:T(8,128)(2,1)S(1)} %get-tuple-element.26.refs_3_, ...), custom_call_target="tpu_custom_call" | custom-call | tf_op jit(solution)/shard_map/relax/pallas_call | solution.py:640
  32.1 0.0 collective-permute-done.5.refs_2_
  32.1 0.8 %rows.1 = f32[9,16,32,256]{3,2,1,0:T(8,128)} custom-call(f32[9,16,32,256]{3,2,1,0:T(8,128)} %bitcast.9, f32[3,16,8,128]{3,2,1,0:T(8,128)S(1)} %get-tuple-element.32.refs_1_, f32[3,16,128]{2,1,0:T(8,128)S(1)} %collective-permute-done.5.refs_2_, f32[16,128]{1,0:T(8,128)S(1)} %get-tuple-element.34.refs_3_), custom_call_target="tpu_custom_call", output_to_operand_aliasing={{}: (0, {})} | custom-call | tf_op jit(solution)/shard_map/rows/pallas_call | solution.py:658
  (4 shorter events, 0.1 us)
Async XLA Ops:
  0.6 27.7 %copy-start = (f32[256]{0:T(256)S(1)}, f32[256]{0:T(256)}, u32[]{:S(2)}) copy-start(f32[256]{0:T(256)} %param.6) | copy-start | bytes 3076
  3.8 4.8 %collective-permute-start = (f32[208,128]{1,0:T(8,128)S(1)}, f32[208,128]{1,0:T(8,128)S(1)}, u32[]{:S(2)}, u32[]{:S(2)}) collective-permute-start(f32[208,128]{1,0:T(8,128)S(1)} %get-tuple-element.19), channel_id=1, source_target_pairs={{0,16},{2,66},{4,20},{6,70},{8,24},{10,74},{12,28},{14,78},{16,0},... | collective-permute-start | bytes 319496 | tf_op jit(solution)/shard_map/ppermute | solution.py:618
  5.4 9.3 %collective-permute-start.2 = (f32[3,32,256]{2,1,0:T(8,128)S(1)}, f32[3,32,256]{2,1,0:T(8,128)S(1)}, u32[]{:S(2)}, u32[]{:S(2)}) collective-permute-start(f32[3,32,256]{2,1,0:T(8,128)S(1)} %get-tuple-element.20), channel_id=1, source_target_pairs={{2,0},{4,2},{6,4},{8,6},{10,8},{12,10},{14,12},{18,16},{20,18},{22... | collective-permute-start | bytes 294920 | tf_op jit(solution)/shard_map/ppermute | solution.py:625
  8.6 6.0 %collective-permute-start.1 = (f32[208,128]{1,0:T(8,128)S(1)}, f32[208,128]{1,0:T(8,128)S(1)}, u32[]{:S(2)}, u32[]{:S(2)}) collective-permute-start(f32[208,128]{1,0:T(8,128)S(1)} %add.14), channel_id=1, source_target_pairs={{0,48},{2,130},{4,52},{6,134},{8,56},{10,138},{12,60},{14,142},{16... | collective-permute-start | bytes 319496 | tf_op jit(solution)/shard_map/ppermute | solution.py:618
  14.7 5.7 %collective-permute-start.3 = (f32[208,128]{1,0:T(8,128)S(1)}, f32[208,128]{1,0:T(8,128)S(1)}, u32[]{:S(2)}, u32[]{:S(2)}) collective-permute-start(f32[208,128]{1,0:T(8,128)S(1)} %select_add_fusion), channel_id=1, source_target_pairs={{0,64},{2,18},{4,68},{6,22},{8,72},{10,26},{12,76},{14,30},{16,80}... | collective-permute-start | bytes 319496 | tf_op jit(solution)/shard_map/ppermute | solution.py:618
  20.5 7.9 %collective-permute-start.4 = (f32[208,128]{1,0:T(8,128)S(1)}, f32[208,128]{1,0:T(8,128)S(1)}, u32[]{:S(2)}, u32[]{:S(2)}) collective-permute-start(f32[208,128]{1,0:T(8,128)S(1)} %add.16.refs_0_), channel_id=1, source_target_pairs={{0,128},{2,50},{4,132},{6,54},{8,136},{10,58},{12,140},{14,62},{16... | collective-permute-start | bytes 319496 | tf_op jit(solution)/shard_map/ppermute | solution.py:618
  23.8 8.2 %collective-permute-start.5 = (f32[3,16,128]{2,1,0:T(8,128)S(1)}, f32[3,16,128]{2,1,0:T(8,128)S(1)}, u32[]{:S(2)}, u32[]{:S(2)}) collective-permute-start(f32[3,16,128]{2,1,0:T(8,128)S(1)} %get-tuple-element.33), channel_id=1, source_target_pairs={{0,1},{1,0},{2,3},{3,2},{4,5},{5,4},{6,7},{7,6},{8,9},{9,8},{10,11... | collective-permute-start | bytes 73736 | tf_op jit(solution)/shard_map/ppermute | solution.py:639

commit v4 on v3

--- a/solution.py
+++ b/solution.py
@@ -623,9 +623,8 @@
     total = sums + partner(sums, steps[0])
     total = jnp.where(swapped, 0.0, total) + partner(total, steps[1])
     halo_x = lax.ppermute(face_x, ("vel", "gx"), upwind_pairs())
-    total, halo_x = lax.optimization_barrier((total, halo_x))
+    total, halo_x, edge_x, edge_y = lax.optimization_barrier((total, halo_x, edge_x, edge_y))
     total = total + partner(total, steps[2])
-    total, edge_x, edge_y = lax.optimization_barrier((total, edge_x, edge_y))
     advected = pl.pallas_call(
         lambda *refs: edges_kernel(wx, wy, *refs),
         out_shape=vmem((9, n, LANES)),

time: 32.9 us -> 35.8 us (1.088); the launches traced: 32.8 us -> 35.2 us
  waiting for transfers between devices: 4.42 us -> 5.97 us
  starting transfers between devices: 16.2 us -> 17.1 us
    ppermute x4, waiting for transfers between devices: 4.42 us -> 5.96 us  [partner(): return lax.ppermute(value, ('vel', 'gx'), pairs)]
    ppermute x1, starting transfers between devices: 4.49 us -> 5.39 us  [shards(): halo_y = lax.ppermute(face_y, 'gy', [(0, 1), (1, 0)])]
  transfers between devices with their start and end apart: 6 -> 6, of which waited for: 2 -> 2; matrix products, arithmetic and copies ran while one was open for 0% -> 0% of each run, Pallas kernels for 23% -> 21%
where the time goes in v4:
time: 35.8 us; the launch traced here: 35.2 us
  starting transfers between devices  17.1 us (48%)
  Pallas kernels  11.3 us (32%)
  waiting for transfers between devices  5.97 us (17%)
  between operations  0.74 us (2%)
    ppermute x4, starting transfers between devices, partner(): return lax.ppermute(value, ('vel', 'gx'), pairs)  9.74 us
    ppermute x4, waiting for transfers between devices, partner(): return lax.ppermute(value, ('vel', 'gx'), pairs)  5.96 us
    ppermute x1, starting transfers between devices, shards(): halo_y = lax.ppermute(face_y, 'gy', [(0, 1), (1, 0)])  5.39 us
    pallas_call x1, Pallas kernels, shards(): pl.pallas_call(lambda *refs: advect_kernel(wx, wy, *refs), out_shape=(vme...  3.7 us
    pallas_call x1, Pallas kernels, shards(): pl.pallas_call(lambda *refs: relax_kernel(wx, wy, *refs), out_shape=(jax....  3.69 us
    pallas_call x1, Pallas kernels, shards(): pl.pallas_call(lambda *refs: moments_kernel(wx, wy, *refs), out_shape=(vm...  3.16 us
    ppermute x1, starting transfers between devices, shards(): halo_x = lax.ppermute(face_x, ('vel', 'gx'), upwind_pairs())  1.93 us
    pallas_call x1, Pallas kernels, shards(): pl.pallas_call(lambda *refs: rows_kernel(wx, wy, *refs), out_shape=jax.Sh...  0.76 us
  transfers between devices with their start and end apart: 6, of which 2 were waited for; matrix products, arithmetic and copies ran while one was open for 0% of the time, Pallas kernels for 21%

profile of v4, /device:TPU:8, one launch (start us, length us, event | category | flops | bytes accessed | tf_op | source)
XLA Modules:
  0.0 35.2 jit_solution(2729207627978535356)
XLA Ops:
  0.6 0.0 copy-start
  0.6 3.2 %moments.1 = (f32[208,128]{1,0:T(8,128)S(1)}, f32[3,32,256]{2,1,0:T(8,128)S(1)}, f32[3,16,128]{2,1,0:T(8,128)S(1)}, f32[16,512]{1,0:T(8,128)S(1)}) custom-call(f32[9,512,256]{2,1,0:T(8,128)} %bitcast.7, s32[64,128]{1,0:T(8,128)} %bitcast.11), custom_call_target="tpu_custom_call" | custom-call | flops 75497472 | bytes 4718592 | tf_op jit(solution)/shard_map/moments/pallas_call | solution.py:576
  3.8 1.6 %collective-permute-start = (f32[208,128]{1,0:T(8,128)S(1)}, f32[208,128]{1,0:T(8,128)S(1)}, u32[]{:S(2)}, u32[]{:S(2)}) collective-permute-start(f32[208,128]{1,0:T(8,128)S(1)} %get-tuple-element.18), channel_id=1, source_target_pairs={{0,16},{2,66},{4,20},{6,70},{8,24},{10,74},{12,28},{14,78},{16,0},... | collective-permute-start | bytes 319496 | tf_op jit(solution)/shard_map/ppermute | solution.py:618
  5.4 1.9 %collective-permute-start.2 = (f32[3,32,256]{2,1,0:T(8,128)S(1)}, f32[3,32,256]{2,1,0:T(8,128)S(1)}, u32[]{:S(2)}, u32[]{:S(2)}) collective-permute-start(f32[3,32,256]{2,1,0:T(8,128)S(1)} %get-tuple-element.19), channel_id=1, source_target_pairs={{2,0},{4,2},{6,4},{8,6},{10,8},{12,10},{14,12},{18,16},{20,18},{22... | collective-permute-start | bytes 294920 | tf_op jit(solution)/shard_map/ppermute | solution.py:625
  7.3 3.7 %advect.1 = (f32[9,512,256]{2,1,0:T(8,128)S(1)}, f32[9,512,256]{2,1,0:T(8,128)S(1)}, f32[32,128]{1,0:T(8,128)S(1)}, f32[16,128]{1,0:T(8,128)S(1)}, bf16[32,640]{1,0:T(8,128)(2,1)S(1)}) custom-call(f32[9,512,256]{2,1,0:T(8,128)} %bitcast.8, bf16[32,640]{1,0:T(8,128)(2,1)} %constant.28.clone.refs_1_, f32[16,512]{1,0:T(8,128)S(1)} %get-tuple-element.20.refs_2_), custom_call_target="tpu_custom_call" | custom-call | flops 23592960 | bytes 14155776 | tf_op jit(solution)/shard_map/advect/pallas_call | solution.py:598
  11.1 0.0 collective-permute-done
  11.1 2.8 %collective-permute-start.1 = (f32[208,128]{1,0:T(8,128)S(1)}, f32[208,128]{1,0:T(8,128)S(1)}, u32[]{:S(2)}, u32[]{:S(2)}) collective-permute-start(f32[208,128]{1,0:T(8,128)S(1)} %add.14), channel_id=1, source_target_pairs={{0,48},{2,130},{4,52},{6,134},{8,56},{10,138},{12,60},{14,142},{16... | collective-permute-start | bytes 319496 | tf_op jit(solution)/shard_map/ppermute | solution.py:618
  13.9 3.1 %collective-permute-done.1 = f32[208,128]{1,0:T(8,128)S(1)} collective-permute-done((f32[208,128]{1,0:T(8,128)S(1)}, f32[208,128]{1,0:T(8,128)S(1)}, u32[]{:S(2)}, u32[]{:S(2)}) %collective-permute-start.1) | collective-permute-done | bytes 106528 | tf_op jit(solution)/shard_map/ppermute | solution.py:618
  17.1 0.1 select_add_fusion
  17.2 0.0 collective-permute-done.2.refs_1_
  17.2 2.0 %collective-permute-start.3 = (f32[208,128]{1,0:T(8,128)S(1)}, f32[208,128]{1,0:T(8,128)S(1)}, u32[]{:S(2)}, u32[]{:S(2)}) collective-permute-start(f32[208,128]{1,0:T(8,128)S(1)} %select_add_fusion), channel_id=1, source_target_pairs={{0,64},{2,18},{4,68},{6,22},{8,72},{10,26},{12,76},{14,30},{16,80}... | collective-permute-start | bytes 319496 | tf_op jit(solution)/shard_map/ppermute | solution.py:618
  19.2 2.8 %collective-permute-done.3 = f32[208,128]{1,0:T(8,128)S(1)} collective-permute-done((f32[208,128]{1,0:T(8,128)S(1)}, f32[208,128]{1,0:T(8,128)S(1)}, u32[]{:S(2)}, u32[]{:S(2)}) %collective-permute-start.3) | collective-permute-done | bytes 106528 | tf_op jit(solution)/shard_map/ppermute | solution.py:618
  22.0 3.3 %collective-permute-start.4 = (f32[208,128]{1,0:T(8,128)S(1)}, f32[208,128]{1,0:T(8,128)S(1)}, u32[]{:S(2)}, u32[]{:S(2)}) collective-permute-start(f32[208,128]{1,0:T(8,128)S(1)} %add.16.refs_0_), channel_id=1, source_target_pairs={{0,128},{2,50},{4,132},{6,54},{8,136},{10,58},{12,140},{14,62},{16... | collective-permute-start | bytes 319496 | tf_op jit(solution)/shard_map/ppermute | solution.py:618
  25.3 5.4 %collective-permute-start.5 = (f32[3,16,128]{2,1,0:T(8,128)S(1)}, f32[3,16,128]{2,1,0:T(8,128)S(1)}, u32[]{:S(2)}, u32[]{:S(2)}) collective-permute-start(f32[3,16,128]{2,1,0:T(8,128)S(1)} %get-tuple-element.31), channel_id=1, source_target_pairs={{0,1},{1,0},{2,3},{3,2},{4,5},{5,4},{6,7},{7,6},{8,9},{9,8},{10,11... | collective-permute-start | bytes 73736 | tf_op jit(solution)/shard_map/ppermute | solution.py:638
  30.7 0.0 copy-done
  30.8 0.0 collective-permute-done.4.refs_1_
  30.8 3.7 %relax.1 = (f32[9,512,256]{2,1,0:T(8,128)}, f32[45,16,32]{2,1,0:T(8,128)}, f32[3,16,8,128]{3,2,1,0:T(8,128)S(1)}) custom-call(f32[208,128]{1,0:T(8,128)S(1)} %add.16.refs_0_, f32[208,128]{1,0:T(8,128)S(1)} %collective-permute-done.4.refs_1_, f32[16,512]{1,0:T(8,128)S(1)} %get-tuple-element.20.refs_2_, bf16[32,640]{1,0:T(8,128)(2,1)S(1)} %get-tuple-element.24.refs_3_, ...), custom_call_target="tpu_custom_call" | custom-call | tf_op jit(solution)/shard_map/relax/pallas_call | solution.py:639
  34.5 0.0 collective-permute-done.5.refs_2_
  34.5 0.8 %rows.1 = f32[9,16,32,256]{3,2,1,0:T(8,128)} custom-call(f32[9,16,32,256]{3,2,1,0:T(8,128)} %bitcast.9, f32[3,16,8,128]{3,2,1,0:T(8,128)S(1)} %get-tuple-element.30.refs_1_, f32[3,16,128]{2,1,0:T(8,128)S(1)} %collective-permute-done.5.refs_2_, f32[16,128]{1,0:T(8,128)S(1)} %get-tuple-element.32.refs_3_), custom_call_target="tpu_custom_call", output_to_operand_aliasing={{}: (0, {})} | custom-call | tf_op jit(solution)/shard_map/rows/pallas_call | solution.py:657
  (4 shorter events, 0.1 us)
Async XLA Ops:
  0.6 30.1 %copy-start = (f32[256]{0:T(256)S(1)}, f32[256]{0:T(256)}, u32[]{:S(2)}) copy-start(f32[256]{0:T(256)} %param.6) | copy-start | bytes 3076
  3.8 7.2 %collective-permute-start = (f32[208,128]{1,0:T(8,128)S(1)}, f32[208,128]{1,0:T(8,128)S(1)}, u32[]{:S(2)}, u32[]{:S(2)}) collective-permute-start(f32[208,128]{1,0:T(8,128)S(1)} %get-tuple-element.18), channel_id=1, source_target_pairs={{0,16},{2,66},{4,20},{6,70},{8,24},{10,74},{12,28},{14,78},{16,0},... | collective-permute-start | bytes 319496 | tf_op jit(solution)/shard_map/ppermute | solution.py:618
  5.4 11.8 %collective-permute-start.2 = (f32[3,32,256]{2,1,0:T(8,128)S(1)}, f32[3,32,256]{2,1,0:T(8,128)S(1)}, u32[]{:S(2)}, u32[]{:S(2)}) collective-permute-start(f32[3,32,256]{2,1,0:T(8,128)S(1)} %get-tuple-element.19), channel_id=1, source_target_pairs={{2,0},{4,2},{6,4},{8,6},{10,8},{12,10},{14,12},{18,16},{20,18},{22... | collective-permute-start | bytes 294920 | tf_op jit(solution)/shard_map/ppermute | solution.py:625
  11.1 6.0 %collective-permute-start.1 = (f32[208,128]{1,0:T(8,128)S(1)}, f32[208,128]{1,0:T(8,128)S(1)}, u32[]{:S(2)}, u32[]{:S(2)}) collective-permute-start(f32[208,128]{1,0:T(8,128)S(1)} %add.14), channel_id=1, source_target_pairs={{0,48},{2,130},{4,52},{6,134},{8,56},{10,138},{12,60},{14,142},{16... | collective-permute-start | bytes 319496 | tf_op jit(solution)/shard_map/ppermute | solution.py:618
  17.2 4.8 %collective-permute-start.3 = (f32[208,128]{1,0:T(8,128)S(1)}, f32[208,128]{1,0:T(8,128)S(1)}, u32[]{:S(2)}, u32[]{:S(2)}) collective-permute-start(f32[208,128]{1,0:T(8,128)S(1)} %select_add_fusion), channel_id=1, source_target_pairs={{0,64},{2,18},{4,68},{6,22},{8,72},{10,26},{12,76},{14,30},{16,80}... | collective-permute-start | bytes 319496 | tf_op jit(solution)/shard_map/ppermute | solution.py:618
  22.0 8.8 %collective-permute-start.4 = (f32[208,128]{1,0:T(8,128)S(1)}, f32[208,128]{1,0:T(8,128)S(1)}, u32[]{:S(2)}, u32[]{:S(2)}) collective-permute-start(f32[208,128]{1,0:T(8,128)S(1)} %add.16.refs_0_), channel_id=1, source_target_pairs={{0,128},{2,50},{4,132},{6,54},{8,136},{10,58},{12,140},{14,62},{16... | collective-permute-start | bytes 319496 | tf_op jit(solution)/shard_map/ppermute | solution.py:618
  25.3 9.1 %collective-permute-start.5 = (f32[3,16,128]{2,1,0:T(8,128)S(1)}, f32[3,16,128]{2,1,0:T(8,128)S(1)}, u32[]{:S(2)}, u32[]{:S(2)}) collective-permute-start(f32[3,16,128]{2,1,0:T(8,128)S(1)} %get-tuple-element.31), channel_id=1, source_target_pairs={{0,1},{1,0},{2,3},{3,2},{4,5},{5,4},{6,7},{7,6},{8,9},{9,8},{10,11... | collective-permute-start | bytes 73736 | tf_op jit(solution)/shard_map/ppermute | solution.py:638
